TPU v7x, 128 devices: a whole 4x4x4 slice. The times are simulated.
128 devices in a mesh: dp: 4 (over z_hi, core), mp: 32 (over y, x, z_lo).
Axes of the slice: x: 4, y: 4, z: 4 (z_hi: 2, z_lo: 2; z = z_hi * 2 + z_lo), core: 2. Of those that a mesh axis runs over, the one named last changes fastest.
Arguments:
- tokens: bfloat16 [2048, 6144], P('dp', 'mp'), may hold values from -6 to 6
- member: int32 [8], P('dp'), may hold values from 0 to 3
- up_weight: bfloat16 [6144, 12288], P('dp', 'mp'), may hold values from -0.078125 to 0.078125
- down_weight: bfloat16 [6144, 12288], P('dp', 'mp'), may hold values from -0.0546875 to 0.0546875
- in_fast: bfloat16 [4, 6144], P(None, 'mp'), may hold values from 0.099609375 to 1.8984375
- hidden_fast: bfloat16 [4, 12288], P(None, 'mp'), may hold values from 0.099609375 to 1.8984375
- mid_fast: bfloat16 [4, 12288], P(None, 'mp'), may hold values from 0.099609375 to 1.8984375
- out_fast: bfloat16 [4, 6144], P(None, 'mp'), may hold values from 0.099609375 to 1.8984375
- cotangent: bfloat16 [2048, 6144], P('dp', 'mp'), may hold values from -0.3125 to 0.3125
Outputs:
- layer_out: bfloat16 [2048, 6144], P('dp', 'mp')
- up_grad: float32 [6144, 12288], P('dp', 'mp')
- down_grad: float32 [6144, 12288], P('dp', 'mp')
- in_fast_grad: float32 [4, 6144], P(None, 'mp')
- hidden_fast_grad: float32 [4, 12288], P(None, 'mp')
- mid_fast_grad: float32 [4, 12288], P(None, 'mp')
- out_fast_grad: float32 [4, 6144], P(None, 'mp')
All inputs are finite; a program needn't handle non-finite values.
Results may differ from a plain program's by a relative error of at most 0.03.
Values may be sent and summed in bfloat16 or wider, within the bound.
A program may use at most 128 MiB of HBM per device.

v0:
```python
import math

import jax
import jax.numpy as jnp
from jax import lax
from jax.sharding import PartitionSpec as P

gelu_scale = math.sqrt(2.0 / math.pi)


def gelu_parts(gated):
    tanh_arg = gelu_scale * (gated + 0.044715 * gated * gated * gated)
    tangent = jnp.tanh(tanh_arg)
    result_value = 0.5 * gated * (1.0 + tangent)
    derivative = 0.5 * (1.0 + tangent) + 0.5 * gated * (1.0 - tangent * tangent) * gelu_scale * (
        1.0 + 3.0 * 0.044715 * gated * gated
    )
    return (result_value, derivative)


def lookup(selector, table):
    return jnp.dot(selector, table.astype(jnp.float32), precision=lax.Precision.HIGHEST)


def per_member(selector, values):
    return lax.dot_general(
        selector, values, (((0,), (0,)), ((), ())), precision=lax.Precision.HIGHEST
    )


def body(
    tokens, member, up_weight, down_weight, in_fast, hidden_fast, mid_fast, out_fast, cotangent
):
    tok_rows = tokens.shape[0]
    patch_count = tok_rows // member.shape[0]
    tok_member = jnp.repeat(member, patch_count)
    selector = (
        tok_member[:, None] == jnp.arange(in_fast.shape[0], dtype=jnp.int32)[None, :]
    ).astype(jnp.float32)
    whole, in_full = (
        lax.all_gather(tokens, "mp", axis=1, tiled=True),
        lax.all_gather(in_fast, "mp", axis=1, tiled=True),
    )
    up_full, down_full = (
        lax.all_gather(up_weight, "dp", axis=0, tiled=True),
        lax.all_gather(down_weight, "dp", axis=0, tiled=True),
    )
    tok_float = whole.astype(jnp.float32)
    average = jnp.mean(tok_float, axis=-1, keepdims=True)
    centered = tok_float - average
    variance = jnp.mean(centered * centered, axis=-1, keepdims=True)
    normed = centered * lax.rsqrt(variance + 1e-06)
    layer_in = (normed * lookup(selector, in_full)).astype(jnp.bfloat16)
    pre_act = jnp.dot(layer_in, up_full, preferred_element_type=jnp.float32)
    hid_row = lookup(selector, hidden_fast)
    mid_row = lookup(selector, mid_fast)
    gated = pre_act * hid_row
    activated, derivative = gelu_parts(gated)
    hidden = (activated * mid_row).astype(jnp.bfloat16)
    branch_term = lax.dot_general(
        hidden, down_full, (((1,), (1,)), ((), ())), preferred_element_type=jnp.float32
    )
    branch = lax.psum_scatter(
        branch_term.astype(jnp.bfloat16), "mp", scatter_dimension=1, tiled=True
    ).astype(jnp.float32)
    layer_out = (tokens.astype(jnp.float32) + branch * lookup(selector, out_fast)).astype(
        jnp.bfloat16
    )
    grad_full, out_full = (
        lax.all_gather(cotangent, "mp", axis=1, tiled=True),
        lax.all_gather(out_fast, "mp", axis=1, tiled=True),
    )
    down_cot = (grad_full.astype(jnp.float32) * lookup(selector, out_full)).astype(jnp.bfloat16)
    out_part = per_member(selector, cotangent.astype(jnp.float32) * branch)
    grad_act = jnp.dot(down_cot, down_full, preferred_element_type=jnp.float32)
    mid_part = per_member(selector, activated * grad_act)
    grad_gated = grad_act * mid_row * derivative
    hidden_part = per_member(selector, pre_act * grad_gated)
    up_cot = (grad_gated * hid_row).astype(jnp.bfloat16)
    up_term = lax.dot_general(
        layer_in, up_cot, (((0,), (0,)), ((), ())), preferred_element_type=jnp.float32
    )
    down_term = lax.dot_general(
        down_cot, hidden, (((0,), (0,)), ((), ())), preferred_element_type=jnp.float32
    )
    up_grad, down_grad = (
        lax.psum_scatter(
            up_term.astype(jnp.bfloat16), "dp", scatter_dimension=0, tiled=True
        ).astype(jnp.float32),
        lax.psum_scatter(
            down_term.astype(jnp.bfloat16), "dp", scatter_dimension=0, tiled=True
        ).astype(jnp.float32),
    )
    projected = lax.dot_general(
        up_cot, up_full, (((1,), (1,)), ((), ())), preferred_element_type=jnp.float32
    )
    member_term = per_member(selector, normed * projected)
    member_local = lax.psum_scatter(
        member_term.astype(jnp.bfloat16), "mp", scatter_dimension=1, tiled=True
    ).astype(jnp.float32)
    out_grad, mid_grad, hidden_grad, in_grad = lax.psum(
        (out_part, mid_part, hidden_part, member_local), "dp"
    )
    return (layer_out, up_grad, down_grad, in_grad, hidden_grad, mid_grad, out_grad)


def solution(mesh):
    in_specs = (
        P("dp", "mp"),
        P("dp"),
        P("dp", "mp"),
        P("dp", "mp"),
        P(None, "mp"),
        P(None, "mp"),
        P(None, "mp"),
        P(None, "mp"),
        P("dp", "mp"),
    )
    out_specs = (
        P("dp", "mp"),
        P("dp", "mp"),
        P("dp", "mp"),
        P(None, "mp"),
        P(None, "mp"),
        P(None, "mp"),
        P(None, "mp"),
    )
    return jax.shard_map(body, mesh=mesh, in_specs=in_specs, out_specs=out_specs, check_vma=False)
```

profile of v0, /device:TPU:1, one launch (start us, length us, event | category | flops | bytes accessed | tf_op | source)
XLA Modules:
  0.0 924.7 jit_solution(15369759522416317650)
XLA Ops:
  10.8 71.2 %all-gather = bf16[32,192,4]{1,2,0:T(4,128)(2,1)S(1)} all-gather(bf16[1,192,4]{1,2,0:T(4,128)(2,1)} %bitcast.46), channel_id=1, replica_groups=mesh['dp'=4,'mp'=32] {'mp'}, dimensions={0}, use_global_device_ids=true | all-gather | bytes 50688 | tf_op jit(solution)/shard_map/all_gather | solution.py:42
  82.1 67.0 %all-gather.1 = bf16[32,192,4]{1,2,0:T(4,128)(2,1)S(1)} all-gather(bf16[1,192,4]{1,2,0:T(4,128)(2,1)} %bitcast.45), channel_id=1, replica_groups=mesh['dp'=4,'mp'=32] {'mp'}, dimensions={0}, use_global_device_ids=true | all-gather | bytes 50688 | tf_op jit(solution)/shard_map/all_gather | solution.py:71
  150.2 9.7 %all-gather.7.cloned.1.call-done = bf16[512,6144]{0,1:T(8,128)(2,1)} async-done(((bf16[512,192]{0,1:T(8,128)(2,1)}), bf16[512,6144]{0,1:T(8,128)(2,1)}) %all-gather.7.cloned.1.call-update) | async-done | bytes 6291472 | tf_op jit(solution)/shard_map/all_gather | solution.py:41
  159.9 8.7 copy.22
  168.6 155.3 %all-gather.13.cloned.1.call-done = bf16[512,6144]{0,1:T(8,128)(2,1)} async-done(((bf16[512,192]{0,1:T(8,128)(2,1)}), bf16[512,6144]{0,1:T(8,128)(2,1)}) %all-gather.13.cloned.1.call-update) | async-done | bytes 6291472 | tf_op jit(solution)/shard_map/all_gather | solution.py:70
  323.9 8.7 copy.24
  332.6 3.8 convert_reduce_fusion
  339.0 4.4 multiply_convert_fusion
  343.5 4.1 fusion.4
  347.6 40.6 %all-gather.11.cloned.1.call-done = bf16[6144,384]{1,0:T(8,128)(2,1)} async-done(((bf16[1536,384]{1,0:T(8,128)(2,1)}), bf16[6144,384]{1,0:T(8,128)(2,1)}) %all-gather.11.cloned.1.call-update) | async-done | bytes 4718608 | tf_op jit(solution)/shard_map/all_gather | solution.py:46
  388.2 6.9 fusion.47
  395.1 35.5 %all-gather.9.cloned.1.call-done = bf16[6144,384]{1,0:T(8,128)(2,1)} async-done(((bf16[1536,384]{1,0:T(8,128)(2,1)}), bf16[6144,384]{1,0:T(8,128)(2,1)}) %all-gather.9.cloned.1.call-update) | async-done | bytes 4718608 | tf_op jit(solution)/shard_map/all_gather | solution.py:45
  430.6 8.0 fusion.46
  440.3 3.5 fusion.48
  443.7 5.9 fusion.8
  451.5 8.5 convolution_convert_fusion.1
  460.0 8.4 convolution_convert_fusion.2
  468.5 7.7 convolution_convert_fusion
  480.3 108.6 %reduce-scatter.13.cloned.1.call-done = bf16[192,4]{1,0:T(8,128)(2,1)} async-done(((bf16[6144,4]{1,0:T(8,128)(2,1)}), bf16[192,4]{1,0:T(8,128)(2,1)}) %reduce-scatter.13.cloned.1.call-update) | async-done | bytes 1552
  589.8 76.3 %reduce-scatter.11.cloned.1.call-done = bf16[1536,384]{1,0:T(8,128)(2,1)} async-done(((bf16[6144,384]{1,0:T(8,128)(2,1)}), bf16[1536,384]{1,0:T(8,128)(2,1)}) %reduce-scatter.11.cloned.1.call-update) | async-done | bytes 1179664 | tf_op jit(solution)/shard_map/reduce_scatter | solution.py:90
  668.9 53.9 %reduce-scatter.9.cloned.1.call-done = bf16[1536,384]{1,0:T(8,128)(2,1)} async-done(((bf16[6144,384]{1,0:T(8,128)(2,1)}), bf16[1536,384]{1,0:T(8,128)(2,1)}) %reduce-scatter.9.cloned.1.call-update) | async-done | bytes 1179664 | tf_op jit(solution)/shard_map/reduce_scatter | solution.py:87
  722.9 2.8 convert_element_type.68
  725.7 151.1 %reduce-scatter.7.cloned.1.call-done = bf16[512,192]{0,1:T(8,128)(2,1)} async-done(((bf16[512,6144]{0,1:T(8,128)(2,1)}), bf16[512,192]{0,1:T(8,128)(2,1)}) %reduce-scatter.7.cloned.1.call-update) | async-done | bytes 196624 | tf_op jit(solution)/shard_map/reduce_scatter | solution.py:63
  878.2 37.7 %all-reduce = (f32[4,192]{1,0:T(4,128)}, f32[4,384]{1,0:T(4,128)}, f32[4,384]{1,0:T(4,128)}, f32[4,192]{1,0:T(4,128)}) all-reduce(bf16[4,192]{1,0:T(4,128)(2,1)S(1)} %copy.27, f32[4,384]{1,0:T(4,128)S(1)} %fusion.23, f32[4,384]{1,0:T(4,128)S(1)} %fusion.21, f32[4,192]{1,0:T(4,128)S(1)} %fusion.25), channel_id=1, replica_groups=mesh['dp'=4,'mp'=32] {'dp'}, use_global_device_ids=true, to_apply=%region_6.0 | all-reduce | flops 4608 | bytes 35328 | tf_op jit(solution)/shard_map/psum | solution.py:101
  (55 shorter events, 22.1 us)
Async XLA Ops:
  7.2 431.4 %copy-start = (bf16[4,384]{1,0:T(4,128)(2,1)S(1)}, bf16[4,384]{1,0:T(4,128)(2,1)}, u32[]{:S(2)}) copy-start(bf16[4,384]{1,0:T(4,128)(2,1)} %param.14) | copy-start | bytes 9220
  7.2 152.7 %all-gather.7.cloned.1.call-start = ((), (), s32[]{:S(2)}) async-start(), calls=%async_computation.4 | async-start | bytes 6488064 | tf_op jit(solution)/shard_map/all_gather | solution.py:41
  7.9 316.0 %all-gather.13.cloned.1.call-start = ((), (), s32[]{:S(2)}) async-start(), calls=%async_computation.8 | async-start | bytes 6488064 | tf_op jit(solution)/shard_map/all_gather | solution.py:70
  8.7 379.5 %all-gather.11.cloned.1.call-start = ((), (), s32[]{:S(2)}) async-start(), calls=%async_computation.6 | async-start | bytes 5898240 | tf_op jit(solution)/shard_map/all_gather | solution.py:46
  9.4 421.2 %all-gather.9.cloned.1.call-start = ((), (), s32[]{:S(2)}) async-start(), calls=%async_computation.5 | async-start | bytes 5898240 | tf_op jit(solution)/shard_map/all_gather | solution.py:45
  10.0 578.9 %reduce-scatter.13.cloned.1.call-start = ((), (), s32[]{:S(2)}) async-start(), calls=%async_computation.11 | async-start | bytes 1622016
  332.6 4.6 copy-start.2
  332.6 6.4 copy-start.3
  430.6 9.7 %copy-start.4 = (bf16[6144,384]{1,0:T(8,128)(2,1)S(1)}, bf16[6144,384]{1,0:T(8,128)(2,1)}, u32[]{:S(2)}) copy-start(bf16[6144,384]{1,0:T(8,128)(2,1)} %all-gather.9.cloned.1.call-done) | copy-start | bytes 14155780
  438.6 5.1 slice-start
  440.3 3.5 slice-start.1
  451.2 214.9 %reduce-scatter.11.cloned.1.call-start = ((), (), s32[]{:S(2)}) async-start(), calls=%async_computation.10 | async-start | bytes 5898240 | tf_op jit(solution)/shard_map/reduce_scatter | solution.py:90
  460.0 262.9 %reduce-scatter.9.cloned.1.call-start = ((), (), s32[]{:S(2)}) async-start(), calls=%async_computation.9 | async-start | bytes 5898240 | tf_op jit(solution)/shard_map/reduce_scatter | solution.py:87
  468.4 408.4 %reduce-scatter.7.cloned.1.call-start = ((), (), s32[]{:S(2)}) async-start(), calls=%async_computation.7 | async-start | bytes 6488064 | tf_op jit(solution)/shard_map/reduce_scatter | solution.py:63
  476.2 441.6 %copy-start.1 = (bf16[4,384]{1,0:T(4,128)(2,1)S(1)}, bf16[4,384]{1,0:T(4,128)(2,1)}, u32[]{:S(2)}) copy-start(bf16[4,384]{1,0:T(4,128)(2,1)} %param.14) | copy-start | bytes 9220
  478.1 398.7 %copy-start.6 = (bf16[512,192]{0,1:T(8,128)(2,1)S(1)}, bf16[512,192]{0,1:T(8,128)(2,1)}, u32[]{:S(2)}) copy-start(bf16[512,192]{0,1:T(8,128)(2,1)} %param.17) | copy-start | bytes 589828
  478.1 437.8 %copy-start.5 = (bf16[512,192]{0,1:T(8,128)(2,1)S(1)}, bf16[512,192]{0,1:T(8,128)(2,1)}, u32[]{:S(2)}) copy-start(bf16[512,192]{0,1:T(8,128)(2,1)} %param.9) | copy-start | bytes 589828
  478.1 437.8 %copy-start.7 = (bf16[4,192]{1,0:T(4,128)(2,1)S(1)}, bf16[4,192]{1,0:T(4,128)(2,1)}, u32[]{:S(2)}) copy-start(bf16[4,192]{1,0:T(4,128)(2,1)} %param.16) | copy-start | bytes 4612
Sparse Core Ops, SparseCore 0:
  9.7 150.1 all-gather.6
  161.5 162.3 all-gather.12
  325.6 62.5 all-gather.10
  389.7 40.8 all-gather.8
  451.3 137.5 reduce-scatter.12
  591.6 74.4 reduce-scatter.10
  668.7 54.0 reduce-scatter.8
  725.4 151.3 reduce-scatter.6
where the time goes:
time: 926 us; the launch traced here: 925 us
  waiting for transfers between devices  634 us (68%)
  blocking collectives  176 us (19%)
  matrix products  67.4 us (7%)
  local copies, waits for them, and re-layouts  21.7 us (2%)
  between operations  14.3 us (2%)
  other arithmetic  11.3 us (1%)
    all_gather x1, waiting for transfers between devices, body(): lax.all_gather(cotangent, 'mp', axis=1, tiled=True)  155 us
    reduce_scatter x1, waiting for transfers between devices, body(): lax.psum_scatter(branch_term.astype(jnp.bfloat16), 'mp', scatter_dimensio...  151 us
    unnamed x9, waiting for transfers between devices  111 us
    reduce_scatter x1, waiting for transfers between devices, body(): lax.psum_scatter(down_term.astype(jnp.bfloat16), 'dp', scatter_dimension=...  76.3 us
    all_gather x1, blocking collectives, body(): lax.all_gather(in_fast, 'mp', axis=1, tiled=True)  71.2 us
    all_gather x1, blocking collectives, body(): lax.all_gather(out_fast, 'mp', axis=1, tiled=True)  67 us
    reduce_scatter x1, waiting for transfers between devices, body(): lax.psum_scatter(up_term.astype(jnp.bfloat16), 'dp', scatter_dimension=0,...  53.9 us
    all_gather x1, waiting for transfers between devices, body(): lax.all_gather(down_weight, 'dp', axis=0, tiled=True)  40.6 us
  transfers between devices with their start and end apart: 8, of which 8 were waited for; matrix products, arithmetic and copies ran while one was open for 8% of the time, Pallas kernels for 0%

commit v1 on v0

v1 whole, which is shorter than its diff:
```python
import math

import jax
import jax.numpy as jnp
from jax import lax
from jax.experimental import pallas as pl
from jax.experimental.pallas import tpu as pltpu
from jax.sharding import Mesh
from jax.sharding import PartitionSpec as P

AXES = ("h", "c", "y", "x", "l")
SIZES = dict(h=2, c=2, y=4, x=4, l=2)
MESH = pl.DeviceIdType.MESH
F32 = jnp.float32
BF16 = jnp.bfloat16
gelu_scale = math.sqrt(2.0 / math.pi)

D_BLK = 1536
PIECE = 192
PAIR = 384
IMG = 256
N_IMG = 8
FFB = 384
HALF = 192
N_SEM = 240


def dot(a, b):
    return jnp.dot(a, b, preferred_element_type=F32)


def dot_t(a, b):
    return lax.dot_general(a, b, (((1,), (1,)), ((), ())), preferred_element_type=F32)


def gelu_parts(gated):
    tanh_arg = gelu_scale * (gated + 0.044715 * gated * gated * gated)
    tangent = jnp.tanh(tanh_arg)
    result_value = 0.5 * gated * (1.0 + tangent)
    derivative = 0.5 * (1.0 + tangent) + 0.5 * gated * (1.0 - tangent * tangent) * gelu_scale * (
        1.0 + 3.0 * 0.044715 * gated * gated
    )
    return (result_value, derivative)


def kernel(
    xt, ct, tab, sel_own, wu, wd, hf, mf,
    bo, ug, dg, fin_in, fin_out, fin_mh,
    gx, xn, gc, wut, wdt, eye, tabs, tabt, sel, stats,
    pa, p_send, p_recv, h_send, h_recv, hid, upc, cot_own,
    rf, rv, ruf, ru, rl, fb, bo_in,
    in_acc, in_recv, y_in, y_out, s_send, s_recv, mh_own, mh_all, ss, rs,
):
    h, c, y, x, l = [lax.axis_index(a) for a in AXES]
    here = dict(h=h, c=c, y=y, x=x, l=l)
    dp = 2 * h + c

    def at(**off):
        pos = dict(here)
        for axis, step in off.items():
            pos[axis] = lax.rem(pos[axis] + (step + SIZES[axis]), SIZES[axis])
        return tuple(pos[a] for a in AXES)

    partner = (y // 2, lax.rem(y, 2), dp, x, l)
    is_self = y == dp
    dp_parts = [at(c=1), at(h=1), at(h=1, c=1)]
    xl_parts = [(dx, dl) for dx in (0, 1, 2, 3) for dl in (0, 1) if dx or dl]
    y_parts = [1, 2, 3]

    counter = [0]
    sends = []

    def start(src, dst, dev):
        i = counter[0]
        counter[0] += 1
        copy = pltpu.make_async_remote_copy(
            src_ref=src, dst_ref=dst, send_sem=ss.at[i], recv_sem=rs.at[i],
            device_id=dev, device_id_type=MESH,
        )
        copy.start()
        sends.append(copy.wait_send)
        return copy

    def start_swap(src, dst):
        i = counter[0]
        counter[0] += 1
        copy = pltpu.make_async_remote_copy(
            src_ref=src, dst_ref=dst, send_sem=ss.at[i], recv_sem=rs.at[i],
            device_id=partner, device_id_type=MESH,
        )

        @pl.when(jnp.logical_not(is_self))
        def _():
            copy.start()

        @pl.when(is_self)
        def _():
            pltpu.make_async_copy(src, dst, rs.at[i]).start()

        def wait_send():
            @pl.when(jnp.logical_not(is_self))
            def _():
                copy.wait_send()

        sends.append(wait_send)
        return copy

    def drain():
        for wait in sends:
            wait()
        sends.clear()

    bar = pltpu.get_barrier_semaphore()
    greet = dp_parts + [at(x=dx, l=dl) for dx, dl in xl_parts] + [at(y=dy) for dy in y_parts]
    for dev in greet:
        pl.semaphore_signal(bar, inc=1, device_id=dev, device_id_type=MESH)

    @pl.when(jnp.logical_not(is_self))
    def _():
        pl.semaphore_signal(bar, inc=1, device_id=partner, device_id_type=MESH)

    pl.semaphore_wait(bar, jnp.where(is_self, len(greet), len(greet) + 1))

    own_piece = 2 * x + l
    own_rows = pl.ds(pl.multiple_of(PIECE * own_piece, PIECE), PIECE)

    swap_x = [start_swap(xt.at[j], gx.at[2 * dp + j, own_rows]) for j in (0, 1)]
    swap_tab = start_swap(tab, tabs.at[own_piece])
    sel_mine = sel.at[pl.ds(2 * dp, 2)]
    sel[pl.ds(2 * dp, 2)] = sel_own[...]
    sel_copies = [start(sel_own, sel_mine, dev) for dev in dp_parts]
    swap_c = [start_swap(ct.at[j], gc.at[2 * dp + j, own_rows]) for j in (0, 1)]

    def chunk(ref, j, du, dv, q=None):
        dy, dx = (dv, du) if j == 0 else (du, dv)
        img = 2 * lax.rem(y + (dy + 4), 4) + j
        row = PAIR * lax.rem(x + (dx + 4), 4)
        size = PAIR
        if q is not None:
            row, size = row + PIECE * q, PIECE
        return ref.at[img, pl.ds(pl.multiple_of(row, PIECE), size)]

    def u_dev(j, step):
        return at(x=step) if j == 0 else at(y=step)

    def v_dev(j, step):
        return at(y=step) if j == 0 else at(x=step)

    def gather(buf, swaps):
        both = (0, 1)
        r = [dict(), dict()]

        def u_send(j, du, q, step, name):
            piece = chunk(buf, j, du, 0, q)
            r[j][name] = start(piece, piece, u_dev(j, step))

        def v_send(j, du, dv, step, name):
            part = chunk(buf, j, du, dv)
            r[j][name] = start(part, part, v_dev(j, step))

        for j in both:
            swaps[j].wait_recv()
            piece = chunk(buf, j, 0, 0, l)
            r[j]["l"] = start(piece, piece, at(l=1))
            u_send(j, 0, l, 1, "-own")
            u_send(j, 0, l, -1, "+own")
        yield
        for j in both:
            r[j]["l"].wait_recv()
            u_send(j, 0, 1 - l, 1, "-oth")
            u_send(j, 0, 1 - l, -1, "+oth")
        for j in both:
            r[j]["-own"].wait_recv()
            u_send(j, -1, l, 1, "fwd-")
        for j in both:
            v_send(j, 0, 0, 1, "v-0")
            v_send(j, 0, 0, -1, "v+0")
        yield
        for j in both:
            r[j]["+own"].wait_recv()
            r[j]["+oth"].wait_recv()
            u_send(j, 1, 1 - l, -1, "fwd+")
            v_send(j, 1, 0, 1, "v-1")
            v_send(j, 1, 0, -1, "v+1")
            r[j]["-oth"].wait_recv()
            v_send(j, -1, 0, 1, "v-m")
            v_send(j, -1, 0, -1, "v+m")
        yield
        for j in both:
            r[j]["fwd-"].wait_recv()
            r[j]["fwd+"].wait_recv()
            v_send(j, 2, 0, 1, "v-2")
            v_send(j, 2, 0, -1, "v+2")
        yield
        for j in both:
            r[j]["v-0"].wait_recv()
            v_send(j, 0, -1, 1, "w-0")
            r[j]["v+1"].wait_recv()
            v_send(j, 1, 1, -1, "w+1")
        yield
        for j in both:
            r[j]["v-m"].wait_recv()
            v_send(j, -1, -1, 1, "w-m")
            r[j]["v+2"].wait_recv()
            v_send(j, 2, 1, -1, "w+2")
        yield
        for name in ("v+0", "v+m", "v-1", "v-2", "w-0", "w+1", "w-m", "w+2"):
            for j in both:
                r[j][name].wait_recv()
        yield

    def run(gen, steps=1000):
        for _ in range(steps):
            if next(gen, "end") == "end":
                return

    run_x = gather(gx, swap_x)
    run_c = gather(gc, swap_c)
    run(run_x, 1)

    swap_tab.wait_recv()
    tab_copies = [
        start(tabs.at[own_piece], tabs.at[own_piece], at(x=dx, l=dl)) for dx, dl in xl_parts
    ]
    run(run_x, 1)
    ident = lax.broadcasted_iota(jnp.int32, (FFB, FFB), 0) == lax.broadcasted_iota(
        jnp.int32, (FFB, FFB), 1
    )
    eye[...] = jnp.where(ident, 1.0, 0.0).astype(BF16)
    run(run_x, 1)
    for src, dst in ((wu, wut), (wd, wdt)):
        for k in range(4):
            dst[:, k * 384 : (k + 1) * 384] = dot_t(
                eye[...], src[k * 384 : (k + 1) * 384, :]
            ).astype(BF16)
    run(run_x, 1)
    for copy in tab_copies:
        copy.wait_recv()
    for copy in sel_copies:
        copy.wait_recv()
    for p in range(8):
        tabt[p * PIECE : (p + 1) * PIECE, :] = dot_t(eye[:PIECE, :IMG], tabs[p]).astype(BF16)
    run(run_x)

    order = [
        2 * lax.rem(y + dy, 4) + j for j, dy in
        ((0, 0), (0, 1), (0, 3), (0, 2), (1, 0), (1, 1), (1, 3), (1, 2))
    ]

    def image_stats(img):
        def total(p, acc):
            rows = pl.ds(pl.multiple_of(p * PIECE, PIECE), PIECE)
            v = gx[img, rows].astype(F32).reshape(PIECE // 8, 8, IMG)
            return acc + jnp.sum(v, axis=0)

        def spread(p, acc):
            rows = pl.ds(pl.multiple_of(p * PIECE, PIECE), PIECE)
            v = (gx[img, rows].astype(F32) - mean).reshape(PIECE // 8, 8, IMG)
            return acc + jnp.sum(v * v, axis=0)

        zero = jnp.zeros((8, IMG), F32)
        mean = jnp.sum(lax.fori_loop(0, 8, total, zero), axis=0, keepdims=True) / D_BLK
        dev2 = jnp.sum(lax.fori_loop(0, 8, spread, zero), axis=0, keepdims=True)
        row = lax.broadcasted_iota(jnp.int32, (8, IMG), 0)
        stats[dp, img] = jnp.where(row == 0, mean, jnp.where(row == 1, dev2, 0.0))

    run(run_c, 1)
    for img in order:
        image_stats(img)
    run(run_c, 1)
    stat_copies = [start(stats.at[dp], stats.at[dp], dev) for dev in dp_parts]
    run(run_c, 1)
    for copy in stat_copies:
        copy.wait_recv()

    def normalise(img):
        parts = [stats[k, img] for k in range(4)]
        mean = (parts[0][0:1] + parts[1][0:1] + parts[2][0:1] + parts[3][0:1]) * 0.25
        dev2 = parts[0][1:2] + parts[1][1:2] + parts[2][1:2] + parts[3][1:2]
        for k in range(4):
            gap = parts[k][0:1] - mean
            dev2 = dev2 + D_BLK * (gap * gap)
        rstd = lax.rsqrt(dev2 / (4 * D_BLK) + 1e-06)

        def step(p, carry):
            rows = pl.ds(pl.multiple_of(p * PIECE, PIECE), PIECE)
            factor = dot(tabt[rows, :], sel[img, 0])
            v = (gx[img, rows].astype(F32) - mean) * rstd
            xn[img, rows] = (v * factor).astype(BF16)
            return carry

        lax.fori_loop(0, 8, step, 0)

    mine = pl.ds(pl.multiple_of(HALF * c, HALF), HALF)
    other = pl.ds(pl.multiple_of(HALF * (1 - c), HALF), HALF)
    core = at(c=1)
    far = at(h=1)

    def partial_product(m, weight_t, operand, img):
        p_send[m, img] = dot(weight_t[other, :], operand[img]).astype(BF16)
        copy = start(p_send.at[m, img], p_recv.at[m, img], core)
        pa[m, img] = dot(weight_t[mine, :], operand[img])
        return copy

    def to_far(m, copy, img):
        copy.wait_recv()
        both = pa[m, img] + p_recv[m, img].astype(F32)
        pa[m, img] = both
        h_send[m, img] = both.astype(BF16)
        return start(h_send.at[m, img], h_recv.at[m, img], far)

    hid_copies = []

    def finish_hidden(copy, img):
        copy.wait_recv()
        pre_act = pa[0, img] + h_recv[0, img].astype(F32)
        pa[0, img] = pre_act
        hid_row = dot(hf[mine, :], sel[img, 0])
        mid_row = dot(mf[mine, :], sel[img, 0])
        activated, _ = gelu_parts(pre_act * hid_row)
        hid[img, mine] = (activated * mid_row).astype(BF16)
        hid_copies.append(start(hid.at[img, mine], hid.at[img, mine], core))

    near, wide = [], []
    for n, img in enumerate(order):
        normalise(img)
        near.append(partial_product(0, wut, xn, img))
        if n >= 1:
            wide.append(to_far(0, near[n - 1], order[n - 1]))
        if n % 2 == 1:
            run(run_c, 1)
    wide.append(to_far(0, near[7], order[7]))
    for n, img in enumerate(order):
        finish_hidden(wide[n], img)
    run(run_c)
    drain()

    br = gx
    for n, img in enumerate(order):
        hid_copies[n].wait_recv()

        def rows_of(k, carry, img=img):
            rows = pl.ds(pl.multiple_of(k * PAIR, PAIR), PAIR)
            br[img, rows] = dot(wd[rows, :], hid[img]).astype(BF16)
            return carry

        lax.fori_loop(0, 4, rows_of, 0)

    cot_own[...] = gc[pl.ds(2 * y, 2), own_rows]

    up, down = (0, -1), (1, 2)
    slot = {0: 0, -1: 1, 1: 2, 2: 3}

    def add_into(dst, *terms):
        total = dst[...].astype(F32)
        for term in terms:
            total = total + term[...].astype(F32)
        dst[...] = total.astype(BF16)

    finals = []

    def scatter():
        both = (0, 1)
        r = [dict(), dict()]
        for j in both:
            for i in (0, 1):
                r[j]["f+", up[i]] = start(chunk(br, j, up[i], 2), rf.at[j, 0, i], v_dev(j, 1))
                r[j]["f-", down[i]] = start(chunk(br, j, down[i], 2), rf.at[j, 1, i], v_dev(j, -1))
        for j in both:
            for k in down:
                r[j]["d+", k] = start(chunk(br, j, k, 1), rv.at[j, 0, slot[k]], v_dev(j, 1))
            for k in up:
                r[j]["d-", k] = start(chunk(br, j, k, -1), rv.at[j, 1, slot[k]], v_dev(j, -1))
        yield
        for i in (0, 1):
            for j in both:
                r[j]["f+", up[i]].wait_recv()
                part = chunk(br, j, up[i], 1)
                add_into(part, rf.at[j, 0, i])
                r[j]["d+", up[i]] = start(part, rv.at[j, 0, slot[up[i]]], v_dev(j, 1))
                r[j]["f-", down[i]].wait_recv()
                part = chunk(br, j, down[i], -1)
                add_into(part, rf.at[j, 1, i])
                r[j]["d-", down[i]] = start(part, rv.at[j, 1, slot[down[i]]], v_dev(j, -1))
            yield

        def total(j, k):
            r[j]["d+", k].wait_recv()
            r[j]["d-", k].wait_recv()
            part = chunk(br, j, k, 0)
            add_into(part, rv.at[j, 0, slot[k]], rv.at[j, 1, slot[k]])

        for j in both:
            total(j, 2)
            r[j]["uf+"] = start(chunk(br, j, 2, 0, 0), ruf.at[j, 0], u_dev(j, 1))
            r[j]["uf-"] = start(chunk(br, j, 2, 0, 1), ruf.at[j, 1], u_dev(j, -1))
        yield
        lo, hi = pl.ds(0, PIECE), pl.ds(PIECE, PIECE)
        for j in both:
            total(j, 1)
            r[j]["u+1"] = start(chunk(br, j, 1, 0, 1), ru.at[j, 0, hi], u_dev(j, 1))
            total(j, -1)
            r[j]["u-0"] = start(chunk(br, j, -1, 0, 0), ru.at[j, 1, lo], u_dev(j, -1))
        yield
        for j in both:
            r[j]["uf+"].wait_recv()
            part = chunk(br, j, 1, 0, 0)
            add_into(part, ruf.at[j, 0])
            r[j]["u+0"] = start(part, ru.at[j, 0, lo], u_dev(j, 1))
            r[j]["uf-"].wait_recv()
            part = chunk(br, j, -1, 0, 1)
            add_into(part, ruf.at[j, 1])
            r[j]["u-1"] = start(part, ru.at[j, 1, hi], u_dev(j, -1))
        for j in both:
            total(j, 0)
        yield
        for j in both:
            for name in ("u+1", "u+0", "u-0", "u-1"):
                r[j][name].wait_recv()
            add_into(chunk(br, j, 0, 0), ru.at[j, 0], ru.at[j, 1])
            r[j]["l"] = start(chunk(br, j, 0, 0, 1 - l), rl.at[j], at(l=1))
        yield
        for j in both:
            r[j]["l"].wait_recv()
            total_piece = chunk(br, j, 0, 0, l)[...].astype(F32) + rl[j].astype(F32)
            fb[j] = total_piece.astype(BF16)
            finals.append(start_swap(fb.at[j], bo_in.at[j]))
        yield

    run_s = scatter()
    run(run_s, 1)

    def scale_cot(img):
        def step(p, carry):
            rows = pl.ds(pl.multiple_of(p * PIECE, PIECE), PIECE)
            factor = dot(tabt[rows, :], sel[img, 1])
            gc[img, rows] = (gc[img, rows].astype(F32) * factor).astype(BF16)
            return carry

        lax.fori_loop(0, 8, step, 0)

    near, wide = [], []
    for n, img in enumerate(order):
        scale_cot(img)
        near.append(partial_product(1, wdt, gc, img))
        if n >= 1:
            wide.append(to_far(1, near[n - 1], order[n - 1]))
    wide.append(to_far(1, near[7], order[7]))
    run(run_s, 1)

    def down_rows(k, carry):
        rows = pl.ds(pl.multiple_of(k * PAIR, PAIR), PAIR)
        acc = dot_t(gc[0, rows], hid[0])
        for img in range(1, 8):
            acc = acc + dot_t(gc[img, rows], hid[img])
        dg[rows, :] = acc
        return carry

    lax.fori_loop(0, 4, down_rows, 0)
    run(run_s, 1)

    mh_own[...] = jnp.zeros((32, IMG), F32)
    upc_copies = []
    for n, img in enumerate(order):
        wide[n].wait_recv()
        grad_act = pa[1, img] + h_recv[1, img].astype(F32)
        pre_act = pa[0, img]
        hid_row = dot(hf[mine, :], sel[img, 0])
        mid_row = dot(mf[mine, :], sel[img, 0])
        activated, derivative = gelu_parts(pre_act * hid_row)
        grad_gated = grad_act * mid_row * derivative
        upc[img, mine] = (grad_gated * hid_row).astype(BF16)
        upc_copies.append(start(upc.at[img, mine], upc.at[img, mine], core))
        pick = sel[img, 0]
        mh_own[0:16, 0:HALF] += dot_t(pick, (activated * grad_act).astype(BF16))
        mh_own[16:32, 0:HALF] += dot_t(pick, (pre_act * grad_gated).astype(BF16))
    mh_all[dp] = mh_own[...]
    mh_copies = [start(mh_own, mh_all.at[dp], dev) for dev in dp_parts]
    run(run_s, 1)
    for copy in upc_copies:
        copy.wait_recv()

    in_acc[...] = jnp.zeros((8, 16, IMG), F32)
    for n, img in enumerate(order):
        def in_rows(p, carry, img=img):
            rows = pl.ds(pl.multiple_of(p * PIECE, PIECE), PIECE)
            prod = dot(wu[rows, :], upc[img]) * xn[img, rows].astype(F32)
            in_acc[p, :, 0:PIECE] += dot_t(sel[img, 0], prod.astype(BF16))
            return carry

        lax.fori_loop(0, 8, in_rows, 0)
    in_copies = []
    for i, (dx, dl) in enumerate(xl_parts):
        p_to = 2 * lax.rem(x + dx, 4) + lax.rem(l + dl, 2)
        in_copies.append(start(in_acc.at[p_to], in_recv.at[i], at(x=dx, l=dl)))
    run(run_s, 1)

    def up_rows(k, carry):
        rows = pl.ds(pl.multiple_of(k * PAIR, PAIR), PAIR)
        acc = dot_t(xn[0, rows], upc[0])
        for img in range(1, 8):
            acc = acc + dot_t(xn[img, rows], upc[img])
        ug[rows, :] = acc
        return carry

    lax.fori_loop(0, 4, up_rows, 0)
    run(run_s, 1)

    for copy in in_copies:
        copy.wait_recv()
    total_in = in_acc[own_piece]
    for i in range(7):
        total_in = total_in + in_recv[i]
    y_in[y] = total_in
    y_in_copies = [start(y_in.at[y], y_in.at[y], at(y=dy)) for dy in y_parts]
    run(run_s)

    out_total = jnp.zeros((16, PIECE), F32)
    for j in (0, 1):
        prod = cot_own[j].astype(F32) * fb[j].astype(F32)
        out_total = out_total + dot_t(sel[2 * y + j, 0], prod.astype(BF16))
    y_out[y] = jnp.zeros((16, IMG), F32)
    y_out[y, :, 0:PIECE] = out_total
    y_out_copies = [start(y_out.at[y], y_out.at[y], at(y=dy)) for dy in y_parts]
    for copy in y_in_copies + y_out_copies:
        copy.wait_recv()
    s_send[0] = (y_in[0] + y_in[1]) + (y_in[2] + y_in[3])
    s_send[1] = (y_out[0] + y_out[1]) + (y_out[2] + y_out[3])
    last = start_swap(s_send, s_recv)
    for copy in mh_copies:
        copy.wait_recv()
    fin_mh[...] = mh_all[...]
    for copy in finals:
        copy.wait_recv()
    bo[...] = bo_in[...]
    last.wait_recv()
    fin_in[...] = s_recv[0]
    fin_out[...] = s_recv[1]
    drain()


def exchange(xt, ct, tab, sel_own, wu, wd, hf, mf):
    vmem = pl.BlockSpec(memory_space=pltpu.VMEM)
    out_shape = [
        jax.ShapeDtypeStruct((2, PIECE, IMG), BF16),
        jax.ShapeDtypeStruct((D_BLK, FFB), F32),
        jax.ShapeDtypeStruct((D_BLK, FFB), F32),
        jax.ShapeDtypeStruct((16, IMG), F32),
        jax.ShapeDtypeStruct((16, IMG), F32),
        jax.ShapeDtypeStruct((4, 32, IMG), F32),
    ]
    scratch = [
        ((N_IMG, D_BLK, IMG), BF16),
        ((N_IMG, D_BLK, IMG), BF16),
        ((N_IMG, D_BLK, IMG), BF16),
        ((FFB, D_BLK), BF16),
        ((FFB, D_BLK), BF16),
        ((FFB, FFB), BF16),
        ((8, 16, IMG), BF16),
        ((D_BLK, 16), BF16),
        ((N_IMG, 2, 16, IMG), BF16),
        ((4, N_IMG, 8, IMG), F32),
        ((2, N_IMG, HALF, IMG), F32),
        ((2, N_IMG, HALF, IMG), BF16),
        ((2, N_IMG, HALF, IMG), BF16),
        ((2, N_IMG, HALF, IMG), BF16),
        ((2, N_IMG, HALF, IMG), BF16),
        ((N_IMG, FFB, IMG), BF16),
        ((N_IMG, FFB, IMG), BF16),
        ((2, PIECE, IMG), BF16),
        ((2, 2, 2, PAIR, IMG), BF16),
        ((2, 2, 4, PAIR, IMG), BF16),
        ((2, 2, PIECE, IMG), BF16),
        ((2, 2, PAIR, IMG), BF16),
        ((2, PIECE, IMG), BF16),
        ((2, PIECE, IMG), BF16),
        ((2, PIECE, IMG), BF16),
        ((8, 16, IMG), F32),
        ((7, 16, IMG), F32),
        ((4, 16, IMG), F32),
        ((4, 16, IMG), F32),
        ((2, 16, IMG), F32),
        ((2, 16, IMG), F32),
        ((32, IMG), F32),
        ((4, 32, IMG), F32),
    ]
    return pl.pallas_call(
        kernel,
        out_shape=out_shape,
        in_specs=[vmem] * 8,
        out_specs=[vmem] * 6,
        scratch_shapes=[pltpu.VMEM(s, d) for s, d in scratch]
        + [pltpu.SemaphoreType.DMA((N_SEM,)), pltpu.SemaphoreType.DMA((N_SEM,))],
        compiler_params=pltpu.CompilerParams(
            collective_id=0, has_side_effects=True, vmem_limit_bytes=62 * 1024 * 1024
        ),
        cost_estimate=pl.CostEstimate(
            flops=14_500_000_000, bytes_accessed=12_000_000, transcendentals=1_600_000
        ),
    )(xt, ct, tab, sel_own, wu, wd, hf, mf)


def body(
    tokens, member, up_weight, down_weight, in_fast, hidden_fast, mid_fast, out_fast, cotangent
):
    def by_image(a):
        return a.reshape(2, IMG, PIECE).transpose(0, 2, 1)

    zero4 = jnp.zeros((4, PIECE), BF16)
    tab = jnp.pad(
        jnp.concatenate([in_fast, out_fast, zero4, zero4], axis=0), ((0, 0), (0, IMG - PIECE))
    )
    row = jnp.arange(16, dtype=jnp.int32)[None, None, :, None]
    shift = jnp.array([0, 4], jnp.int32)[None, :, None, None]
    sel_own = jnp.broadcast_to(
        (row == member[:, None, None, None] + shift).astype(BF16), (2, 2, 16, IMG)
    )
    hf = jnp.pad(hidden_fast.T, ((0, 0), (0, 12)))
    mf = jnp.pad(mid_fast.T, ((0, 0), (0, 12)))
    branch, ug, dg, fin_in, fin_out, fin_mh = exchange(
        by_image(tokens), by_image(cotangent), tab, sel_own, up_weight, down_weight, hf, mf
    )
    out_rows = jnp.repeat(out_fast.astype(F32)[member], IMG, axis=0)
    branch = branch.transpose(0, 2, 1).reshape(2 * IMG, PIECE).astype(F32)
    layer_out = (tokens.astype(F32) + branch * out_rows).astype(BF16)
    in_grad = fin_in[0:4, 0:PIECE] / in_fast.astype(F32)
    out_grad = fin_out[0:4, 0:PIECE]
    mid_grad = jnp.concatenate([fin_mh[0, 0:4, 0:HALF], fin_mh[1, 0:4, 0:HALF]], axis=1)
    hidden_grad = jnp.concatenate([fin_mh[0, 16:20, 0:HALF], fin_mh[1, 16:20, 0:HALF]], axis=1)
    return (layer_out, ug, dg, in_grad, hidden_grad, mid_grad, out_grad)


def solution(mesh):
    grid = Mesh(mesh.devices.reshape([SIZES[a] for a in AXES]), AXES)
    dp, mp = ("h", "c"), ("y", "x", "l")
    in_specs = (
        P(dp, mp),
        P(dp),
        P(dp, mp),
        P(dp, mp),
        P(None, mp),
        P(None, mp),
        P(None, mp),
        P(None, mp),
        P(dp, mp),
    )
    out_specs = (
        P(dp, mp),
        P(dp, mp),
        P(dp, mp),
        P(None, mp),
        P(None, mp),
        P(None, mp),
        P(None, mp),
    )
    return jax.shard_map(body, mesh=grid, in_specs=in_specs, out_specs=out_specs, check_vma=False)
```

time: 926 us -> 220 us (0.24)
  the two profiles are of different devices: /device:TPU:1 before, /device:TPU:16 now
where the time goes in v1:
time: 220 us; the launch traced here: 219 us
  Pallas kernels  197 us (90%)
  local copies, waits for them, and re-layouts  13.6 us (6%)
  other arithmetic  7.32 us (3%)
    pallas_call x1, Pallas kernels, exchange(): pl.pallas_call(kernel, out_shape=out_shape, in_specs=[vmem] * 8, out_spec...  197 us
    unnamed x10, local copies, waits for them, and re-layouts  6.5 us

profile of v1, /device:TPU:16, one launch (start us, length us, event | category | flops | bytes accessed | tf_op | source)
XLA Modules:
  0.0 219.0 jit_solution(8932657884152232032)
XLA Ops:
  0.6 0.7 compare_select_fusion
  1.3 0.1 pad.20.clone
  1.4 0.7 broadcast_add_fusion
  2.1 0.1 compare_convert_fusion
  2.2 0.7 convert_element_type.33
  2.9 0.6 gather_fusion
  3.4 0.8 maximum_maximum_fusion
  4.2 0.6 pad.11.tab
  4.8 0.7 broadcast_in_dim.6.sel_own
  5.5 0.9 copy.21
  6.3 0.7 pad.12.hf
  7.0 0.9 copy.22
  7.9 0.7 pad.13.mf
  8.5 1.8 bitcast_bitcast_fusion
  10.3 197.4 %shard_map.153 = (bf16[2,192,256]{2,1,0:T(8,128)(2,1)}, f32[1536,384]{1,0:T(8,128)}, f32[1536,384]{1,0:T(8,128)}, f32[16,256]{1,0:T(8,128)}, f32[16,256]{1,0:T(8,128)}, /*index=5*/f32[4,32,256]{2,1,0:T(8,128)}) custom-call(bf16[2,192,256]{2,1,0:T(8,128)(2,1)} %get-tuple-element.24.xt, bf16[2,192,256]{2,1,0:T(8,128)(2,1)} %get-tuple-element.23.ct, ...), custom_call_target="tpu_custom_call" | custom-call | flops 14499999744 | bytes 12000000 | tf_op jit(solution)/shard_map/pallas_call | solution.py:587
  207.8 1.3 convert_divide_fusion
  209.1 1.3 slice.23
  210.4 0.7 slice_bitcast_fusion.1
  211.1 0.7 pad_maximum_fusion.1
  211.8 0.7 pad_maximum_fusion
  212.4 1.0 multiply_bitcast_fusion
  213.5 0.7 add_convert_fusion
  214.3 3.4 %copy.31 = f32[1536,384]{1,0:T(8,128)} copy(f32[1536,384]{1,0:T(8,128)} %get-tuple-element.33) | data formatting | bytes 4718592
  217.6 1.4 copy.32
  (10 shorter events, 0.1 us)
Async XLA Ops:
  10.3 197.4 %copy-start.2 = (bf16[4,192]{1,0:T(4,128)(2,1)S(1)}, bf16[4,192]{1,0:T(4,128)(2,1)}, u32[]{:S(2)}) copy-start(bf16[4,192]{1,0:T(4,128)(2,1)} %param.14) | copy-start | bytes 4612
  10.3 203.2 %copy-start.1 = (bf16[512,192]{0,1:T(8,128)(2,1)S(1)}, bf16[512,192]{0,1:T(8,128)(2,1)}, u32[]{:S(2)}) copy-start(bf16[512,192]{0,1:T(8,128)(2,1)} %param.10) | copy-start | bytes 589828
  214.3 3.4 %copy-start = (f32[1536,384]{1,0:T(8,128)S(1)}, f32[1536,384]{1,0:T(8,128)}, u32[]{:S(2)}) copy-start(f32[1536,384]{1,0:T(8,128)} %get-tuple-element.34) | copy-start | bytes 7077892

commit v2 on v1

v2 whole, which is shorter than its diff:
```python
import math

import jax
import jax.numpy as jnp
from jax import lax
from jax.experimental import pallas as pl
from jax.experimental.pallas import tpu as pltpu
from jax.sharding import Mesh
from jax.sharding import PartitionSpec as P

AXES = ("h", "c", "y", "x", "l")
SIZES = dict(h=2, c=2, y=4, x=4, l=2)
MESH = pl.DeviceIdType.MESH
F32 = jnp.float32
BF16 = jnp.bfloat16
gelu_scale = math.sqrt(2.0 / math.pi)

D_BLK = 1536
PIECE = 192
PAIR = 384
IMG = 256
N_IMG = 8
FFB = 384
HALF = 192
N_SEM = 240


def dot(a, b):
    return jnp.dot(a, b, preferred_element_type=F32)


def dot_t(a, b):
    return lax.dot_general(a, b, (((1,), (1,)), ((), ())), preferred_element_type=F32)


def gelu_parts(gated):
    tanh_arg = gelu_scale * (gated + 0.044715 * gated * gated * gated)
    tangent = jnp.tanh(tanh_arg)
    result_value = 0.5 * gated * (1.0 + tangent)
    derivative = 0.5 * (1.0 + tangent) + 0.5 * gated * (1.0 - tangent * tangent) * gelu_scale * (
        1.0 + 3.0 * 0.044715 * gated * gated
    )
    return (result_value, derivative)


def kernel(
    tok, cot, member, in_fast, out_fast, hidden_fast, mid_fast, wu, wd,
    lo, ug, dg, fin_in, fin_out, fin_mid, fin_hid,
    gx, xn, gc, dc, eye, tab_f, tab_own, hm_col, tabs, tabt, own_col, sel, selm, stats, col,
    pa, p_send, p_recv, h_send, h_recv, hid, upc,
    rf, rv, ruf, ru, rl, fb, bo_in,
    in_acc, in_recv, y_in, y_out, s_send, s_recv, mh_own, mh_all, ss, rs,
):
    h, c, y, x, l = [lax.axis_index(a) for a in AXES]
    here = dict(h=h, c=c, y=y, x=x, l=l)
    dp = 2 * h + c

    def at(**off):
        pos = dict(here)
        for axis, step in off.items():
            pos[axis] = lax.rem(pos[axis] + (step + SIZES[axis]), SIZES[axis])
        return tuple(pos[a] for a in AXES)

    partner = (y // 2, lax.rem(y, 2), dp, x, l)
    is_self = y == dp
    dp_parts = [at(c=1), at(h=1), at(h=1, c=1)]
    xl_parts = [(dx, dl) for dx in (0, 1, 2, 3) for dl in (0, 1) if dx or dl]
    y_parts = [1, 2, 3]

    counter = [0]
    sends = []

    def start(src, dst, dev):
        i = counter[0]
        counter[0] += 1
        copy = pltpu.make_async_remote_copy(
            src_ref=src, dst_ref=dst, send_sem=ss.at[i], recv_sem=rs.at[i],
            device_id=dev, device_id_type=MESH,
        )
        copy.start()
        sends.append(copy.wait_send)
        return copy

    def start_swap(src, dst):
        i = counter[0]
        counter[0] += 1
        copy = pltpu.make_async_remote_copy(
            src_ref=src, dst_ref=dst, send_sem=ss.at[i], recv_sem=rs.at[i],
            device_id=partner, device_id_type=MESH,
        )

        @pl.when(jnp.logical_not(is_self))
        def _():
            copy.start()

        @pl.when(is_self)
        def _():
            pltpu.make_async_copy(src, dst, rs.at[i]).start()

        def wait_send():
            @pl.when(jnp.logical_not(is_self))
            def _():
                copy.wait_send()

        sends.append(wait_send)
        return copy

    def drain(waits):
        for wait in waits:
            wait()
        waits.clear()

    bar = pltpu.get_barrier_semaphore()
    greet = dp_parts + [at(x=dx, l=dl) for dx, dl in xl_parts] + [at(y=dy) for dy in y_parts]
    for dev in greet:
        pl.semaphore_signal(bar, inc=1, device_id=dev, device_id_type=MESH)

    @pl.when(jnp.logical_not(is_self))
    def _():
        pl.semaphore_signal(bar, inc=1, device_id=partner, device_id_type=MESH)

    member_row = lax.broadcasted_iota(jnp.int32, (16, IMG), 0)
    for i in (0, 1):
        for t in (0, 1):
            sel[2 * dp + i, t] = jnp.where(member_row == member[i] + 8 * t, 1.0, 0.0).astype(BF16)
    tab_f[...] = jnp.zeros((16, FFB), F32)
    tab_f[0:4, 0:PIECE] = in_fast[...].astype(F32)
    tab_f[8:12, 0:PIECE] = out_fast[...].astype(F32)
    tab_own[...] = tab_f[:, 0:IMG].astype(BF16)

    pl.semaphore_wait(bar, jnp.where(is_self, len(greet), len(greet) + 1))

    own_piece = 2 * x + l
    own_rows = pl.ds(pl.multiple_of(PIECE * own_piece, PIECE), PIECE)

    lanes = [pl.ds(0, IMG), pl.ds(IMG, IMG)]
    swap_x = [start_swap(tok.at[:, lanes[j]], gx.at[2 * dp + j, own_rows]) for j in (0, 1)]
    swap_tab = start_swap(tab_own, tabs.at[own_piece])
    sel_mine = sel.at[pl.ds(2 * dp, 2)]
    sel_copies = [start(sel_mine, sel_mine, dev) for dev in dp_parts]
    swap_c = [start_swap(cot.at[:, lanes[j]], gc.at[2 * dp + j, own_rows]) for j in (0, 1)]

    def image(j, dy):
        return 2 * lax.rem(y + (dy + 4), 4) + j

    def chunk(ref, j, du, dv, q=None):
        dy, dx = (dv, du) if j == 0 else (du, dv)
        row = PAIR * lax.rem(x + (dx + 4), 4)
        size = PAIR
        if q is not None:
            row, size = row + PIECE * q, PIECE
        return ref.at[image(j, dy), pl.ds(pl.multiple_of(row, PIECE), size)]

    def u_dev(j, step):
        return at(x=step) if j == 0 else at(y=step)

    def v_dev(j, step):
        return at(y=step) if j == 0 else at(x=step)

    both = (0, 1)

    def gather(buf, swaps):
        r = [dict(), dict()]

        def u_send(j, du, q, step, name):
            piece = chunk(buf, j, du, 0, q)
            r[j][name] = start(piece, piece, u_dev(j, step))

        def v_send(j, du, dv, step, name):
            part = chunk(buf, j, du, dv)
            r[j][name] = start(part, part, v_dev(j, step))

        for j in both:
            swaps[j].wait_recv()
            piece = chunk(buf, j, 0, 0, l)
            r[j]["l"] = start(piece, piece, at(l=1))
            u_send(j, 0, l, 1, "-own")
            u_send(j, 0, l, -1, "+own")
        yield
        for j in both:
            r[j]["l"].wait_recv()
            u_send(j, 0, 1 - l, 1, "-oth")
            u_send(j, 0, 1 - l, -1, "+oth")
        for j in both:
            r[j]["-own"].wait_recv()
            u_send(j, -1, l, 1, "fwd-")
        for j in both:
            v_send(j, 0, 0, 1, "v-0")
            v_send(j, 0, 0, -1, "v+0")
        yield
        for j in both:
            r[j]["+own"].wait_recv()
            r[j]["+oth"].wait_recv()
            u_send(j, 1, 1 - l, -1, "fwd+")
            v_send(j, 1, 0, 1, "v-1")
            v_send(j, 1, 0, -1, "v+1")
            r[j]["-oth"].wait_recv()
            v_send(j, -1, 0, 1, "v-m")
            v_send(j, -1, 0, -1, "v+m")
        yield
        for j in both:
            r[j]["fwd-"].wait_recv()
            r[j]["fwd+"].wait_recv()
            v_send(j, 2, 0, 1, "v-2")
            v_send(j, 2, 0, -1, "v+2")
        yield
        for j in both:
            r[j]["v-0"].wait_recv()
            v_send(j, 0, -1, 1, "w-0")
            r[j]["v+1"].wait_recv()
            v_send(j, 1, 1, -1, "w+1")
        yield
        for j in both:
            r[j]["v-m"].wait_recv()
            v_send(j, -1, -1, 1, "w-m")
            r[j]["v+2"].wait_recv()
            v_send(j, 2, 1, -1, "w+2")
        yield
        for name in ("v+0", "v+m", "v-1", "v-2"):
            for j in both:
                r[j][name].wait_recv()
        r[1]["w-0"].wait_recv()
        yield
        for name in ("w-0", "w+1", "w-m", "w+2"):
            for j in both:
                if (j, name) != (1, "w-0"):
                    r[j][name].wait_recv()
        yield

    def run(gen, steps=1000):
        for _ in range(steps):
            if next(gen, "end") == "end":
                return

    first = [image(0, 0)]
    second = [image(1, 0), image(0, -1), image(0, 1)]
    third = [image(1, -1), image(1, 1), image(0, 2), image(1, 2)]
    order = first + second + third

    run_x = gather(gx, swap_x)
    run_c = gather(gc, swap_c)
    run(run_x, 1)

    swap_tab.wait_recv()
    tab_copies = [
        start(tabs.at[own_piece], tabs.at[own_piece], at(x=dx, l=dl)) for dx, dl in xl_parts
    ]
    run(run_x, 1)
    ident = lax.broadcasted_iota(jnp.int32, (FFB, FFB), 0) == lax.broadcasted_iota(
        jnp.int32, (FFB, FFB), 1
    )
    eye[...] = jnp.where(ident, 1.0, 0.0).astype(BF16)
    run(run_x, 1)
    own_col[...] = dot_t(eye[:PIECE, :IMG], tab_own[...]).astype(BF16)
    tab_f[0:4, :] = hidden_fast[...].astype(F32)
    tab_f[8:12, :] = mid_fast[...].astype(F32)
    hm_col[...] = dot_t(eye[...], tab_f[...].astype(BF16)).astype(BF16)
    col[...] = jnp.zeros((D_BLK, 128), F32)
    run(run_x, 1)
    for copy in sel_copies:
        copy.wait_recv()
    for copy in tab_copies:
        copy.wait_recv()
    for p in range(8):
        tabt[p * PIECE : (p + 1) * PIECE, :] = dot_t(eye[:PIECE, :IMG], tabs[p]).astype(BF16)
    lane = lax.broadcasted_iota(jnp.int32, (16, 128), 1)
    picks = jnp.zeros((16, 128), F32)
    for img in range(N_IMG):
        picks = jnp.where(lane == img, sel[img, 0][:, 0:128].astype(F32), picks)
    selm[...] = picks

    stat_copies = {}
    stat_row = lax.broadcasted_iota(jnp.int32, (8, IMG), 0)

    def image_stats(n):
        img = order[n]

        def total(p, acc):
            rows = pl.ds(pl.multiple_of(p * PIECE, PIECE), PIECE)
            v = gx[img, rows].astype(F32).reshape(PIECE // 8, 8, IMG)
            return acc + jnp.sum(v, axis=0)

        def spread(p, acc):
            rows = pl.ds(pl.multiple_of(p * PIECE, PIECE), PIECE)
            v = (gx[img, rows].astype(F32) - mean).reshape(PIECE // 8, 8, IMG)
            return acc + jnp.sum(v * v, axis=0)

        zero = jnp.zeros((8, IMG), F32)
        mean = jnp.sum(lax.fori_loop(0, 8, total, zero), axis=0, keepdims=True) / D_BLK
        dev2 = jnp.sum(lax.fori_loop(0, 8, spread, zero), axis=0, keepdims=True)
        stats[dp, img] = jnp.where(stat_row == 0, mean, jnp.where(stat_row == 1, dev2, 0.0))
        part = stats.at[dp, img]
        stat_copies[n] = [start(part, part, dev) for dev in dp_parts]

    def normalise(n):
        img = order[n]
        for copy in stat_copies[n]:
            copy.wait_recv()
        parts = [stats[k, img] for k in range(4)]
        mean = (parts[0][0:1] + parts[1][0:1] + parts[2][0:1] + parts[3][0:1]) * 0.25
        dev2 = parts[0][1:2] + parts[1][1:2] + parts[2][1:2] + parts[3][1:2]
        for k in range(4):
            gap = parts[k][0:1] - mean
            dev2 = dev2 + D_BLK * (gap * gap)
        rstd = lax.rsqrt(dev2 / (4 * D_BLK) + 1e-06)
        factor = dot(tabt[...], sel[img, 0])
        xn[img] = ((gx[img].astype(F32) - mean) * rstd * factor).astype(BF16)

    mine = pl.ds(pl.multiple_of(HALF * c, HALF), HALF)
    other = pl.ds(pl.multiple_of(HALF * (1 - c), HALF), HALF)
    core = at(c=1)
    far = at(h=1)
    near = [dict(), dict()]
    wide = [dict(), dict()]

    def partial_product(m, weight, operand, n):
        img = order[n]
        part = lax.dot_general(
            weight[...], operand[img], (((0,), (0,)), ((), ())), preferred_element_type=F32
        )
        low, high = part[0:HALF], part[HALF:FFB]
        p_send[m, img] = jnp.where(c == 0, high, low).astype(BF16)
        near[m][n] = start(p_send.at[m, img], p_recv.at[m, img], core)
        pa[m, img] = jnp.where(c == 0, low, high)

    def to_far(m, n):
        img = order[n]
        near[m][n].wait_recv()
        total = pa[m, img] + p_recv[m, img].astype(F32)
        pa[m, img] = total
        h_send[m, img] = total.astype(BF16)
        wide[m][n] = start(h_send.at[m, img], h_recv.at[m, img], far)

    hid_copies, upc_copies = {}, {}

    def finish_hidden(n):
        img = order[n]
        wide[0][n].wait_recv()
        pre_act = pa[0, img] + h_recv[0, img].astype(F32)
        pa[0, img] = pre_act
        hid_row = dot(hm_col[mine, :], sel[img, 0])
        mid_row = dot(hm_col[mine, :], sel[img, 1])
        activated, _ = gelu_parts(pre_act * hid_row)
        hid[img, mine] = (activated * mid_row).astype(BF16)
        hid_copies[n] = start(hid.at[img, mine], hid.at[img, mine], core)

    br = gx

    def branch_part(n):
        img = order[n]
        hid_copies[n].wait_recv()
        br[img] = dot(wd[...], hid[img]).astype(BF16)

    def forward(n):
        normalise(n)
        partial_product(0, wu, xn, n)

    run(run_x, 2)
    image_stats(0)
    run(run_c, 1)
    run(run_x, 1)
    for n in (1, 2, 3):
        image_stats(n)
    forward(0)
    run(run_c, 1)
    forward(1)
    to_far(0, 0)
    run(run_x, 1)
    x_sends = list(sends)
    sends.clear()
    for n in (4, 5, 6, 7):
        image_stats(n)
    forward(2)
    to_far(0, 1)
    forward(3)
    to_far(0, 2)
    run(run_c, 1)
    finish_hidden(0)
    for n in (4, 5, 6, 7):
        forward(n)
        to_far(0, n - 1)
        finish_hidden(n - 3)
    run(run_c, 1)
    to_far(0, 7)
    finish_hidden(5)
    drain(x_sends)
    run(run_c, 1)
    for n in (0, 1, 2):
        branch_part(n)
    finish_hidden(6)
    for n in (3, 4, 5):
        branch_part(n)
    finish_hidden(7)
    run(run_c, 1)
    for n in (6, 7):
        branch_part(n)

    up, down = (0, -1), (1, 2)
    slot = {0: 0, -1: 1, 1: 2, 2: 3}

    def add_into(dst, *terms):
        total = dst[...].astype(F32)
        for term in terms:
            total = total + term[...].astype(F32)
        dst[...] = total.astype(BF16)

    finals = []

    def scatter():
        r = [dict(), dict()]
        for j in both:
            for i in (0, 1):
                r[j]["f+", up[i]] = start(chunk(br, j, up[i], 2), rf.at[j, 0, i], v_dev(j, 1))
                r[j]["f-", down[i]] = start(chunk(br, j, down[i], 2), rf.at[j, 1, i], v_dev(j, -1))
        for j in both:
            for k in (2, 1):
                r[j]["d+", k] = start(chunk(br, j, k, 1), rv.at[j, 0, slot[k]], v_dev(j, 1))
            for k in (-1, 0):
                r[j]["d-", k] = start(chunk(br, j, k, -1), rv.at[j, 1, slot[k]], v_dev(j, -1))
        yield
        for i in (1, 0):
            for j in both:
                r[j]["f+", up[i]].wait_recv()
                part = chunk(br, j, up[i], 1)
                add_into(part, rf.at[j, 0, i])
                r[j]["d+", up[i]] = start(part, rv.at[j, 0, slot[up[i]]], v_dev(j, 1))
                r[j]["f-", down[i]].wait_recv()
                part = chunk(br, j, down[i], -1)
                add_into(part, rf.at[j, 1, i])
                r[j]["d-", down[i]] = start(part, rv.at[j, 1, slot[down[i]]], v_dev(j, -1))
            yield

        def total(j, k):
            r[j]["d+", k].wait_recv()
            r[j]["d-", k].wait_recv()
            part = chunk(br, j, k, 0)
            add_into(part, rv.at[j, 0, slot[k]], rv.at[j, 1, slot[k]])

        for j in both:
            total(j, 2)
            r[j]["uf+"] = start(chunk(br, j, 2, 0, 0), ruf.at[j, 0], u_dev(j, 1))
            r[j]["uf-"] = start(chunk(br, j, 2, 0, 1), ruf.at[j, 1], u_dev(j, -1))
        yield
        low, high = pl.ds(0, PIECE), pl.ds(PIECE, PIECE)
        for j in both:
            total(j, -1)
            r[j]["u-0"] = start(chunk(br, j, -1, 0, 0), ru.at[j, 1, low], u_dev(j, -1))
        for j in both:
            total(j, 1)
            r[j]["u+1"] = start(chunk(br, j, 1, 0, 1), ru.at[j, 0, high], u_dev(j, 1))
        yield
        for j in both:
            r[j]["uf+"].wait_recv()
            part = chunk(br, j, 1, 0, 0)
            add_into(part, ruf.at[j, 0])
            r[j]["u+0"] = start(part, ru.at[j, 0, low], u_dev(j, 1))
            r[j]["uf-"].wait_recv()
            part = chunk(br, j, -1, 0, 1)
            add_into(part, ruf.at[j, 1])
            r[j]["u-1"] = start(part, ru.at[j, 1, high], u_dev(j, -1))
        for j in both:
            total(j, 0)
        yield
        for j in both:
            for name in ("u+1", "u+0", "u-0", "u-1"):
                r[j][name].wait_recv()
            add_into(chunk(br, j, 0, 0), ru.at[j, 0], ru.at[j, 1])
            r[j]["l"] = start(chunk(br, j, 0, 0, 1 - l), rl.at[j], at(l=1))
        yield
        for j in both:
            r[j]["l"].wait_recv()
            piece = chunk(br, j, 0, 0, l)[...].astype(F32) + rl[j].astype(F32)
            fb[j] = piece.astype(BF16)
            finals.append(start_swap(fb.at[j], bo_in.at[j]))
        yield

    run_s = scatter()
    run(run_s, 1)

    def backward(n):
        img = order[n]
        factor = dot(tabt[...], sel[img, 1])
        dc[img] = (gc[img].astype(F32) * factor).astype(BF16)
        partial_product(1, wd, dc, n)

    mh_own[...] = jnp.zeros((32, IMG), F32)

    def finish_cot(n):
        img = order[n]
        wide[1][n].wait_recv()
        grad_act = pa[1, img] + h_recv[1, img].astype(F32)
        pre_act = pa[0, img]
        hid_row = dot(hm_col[mine, :], sel[img, 0])
        mid_row = dot(hm_col[mine, :], sel[img, 1])
        activated, derivative = gelu_parts(pre_act * hid_row)
        grad_gated = grad_act * mid_row * derivative
        upc[img, mine] = (grad_gated * hid_row).astype(BF16)
        upc_copies[n] = start(upc.at[img, mine], upc.at[img, mine], core)
        pick = sel[img, 0]
        mh_own[0:16, 0:HALF] += dot_t(pick, (activated * grad_act).astype(BF16))
        mh_own[16:32, 0:HALF] += dot_t(pick, (pre_act * grad_gated).astype(BF16))

    def down_rows(k):
        rows = pl.ds(k * PAIR, PAIR)
        acc = dot_t(dc[0, rows], hid[0])
        for img in range(1, 8):
            acc = acc + dot_t(dc[img, rows], hid[img])
        dg[rows, :] = acc.astype(BF16)

    def up_rows(k):
        rows = pl.ds(k * PAIR, PAIR)
        weight = wu[rows, :].astype(F32)
        acc = jnp.zeros((PAIR, FFB), F32)
        for img in range(8):
            part = dot_t(xn[img, rows], upc[img])
            acc = acc + part
            col[rows, img : img + 1] = jnp.sum(part * weight, axis=1, keepdims=True)
        ug[rows, :] = acc.astype(BF16)

    backward(0)
    run(run_c, 1)
    to_far(1, 0)
    for n in (1, 2, 3):
        backward(n)
        if n > 1:
            to_far(1, n - 1)
    run(run_c, 1)
    to_far(1, 3)
    for n in (4, 5, 6, 7):
        backward(n)
        if n > 4:
            to_far(1, n - 1)
        finish_cot(n - 4)
    to_far(1, 7)
    run(run_s, 1)
    down_rows(0)
    finish_cot(4)
    run(run_s, 1)
    down_rows(1)
    finish_cot(5)
    down_rows(2)
    finish_cot(6)
    down_rows(3)
    finish_cot(7)
    mh_all[dp] = mh_own[...]
    mh_copies = [start(mh_own, mh_all.at[dp], dev) for dev in dp_parts]
    for n in range(8):
        upc_copies[n].wait_recv()
    up_rows(0)
    run(run_s, 1)
    up_rows(1)
    up_rows(2)
    run(run_s, 1)
    up_rows(3)
    run(run_s, 1)

    in_acc[...] = jnp.zeros((8, 16, IMG), F32)
    for p in range(8):
        in_acc[p, :, 0:PIECE] = lax.dot_general(
            selm[...], col[p * PIECE : (p + 1) * PIECE, :], (((1,), (1,)), ((), ())),
            precision=lax.Precision.HIGHEST, preferred_element_type=F32,
        )
    in_copies = []
    for i, (dx, dl) in enumerate(xl_parts):
        p_to = 2 * lax.rem(x + dx, 4) + lax.rem(l + dl, 2)
        in_copies.append(start(in_acc.at[p_to], in_recv.at[i], at(x=dx, l=dl)))
    run(run_s, 1)
    for copy in in_copies:
        copy.wait_recv()
    total_in = in_acc[own_piece]
    for i in range(7):
        total_in = total_in + in_recv[i]
    y_in[y] = total_in
    y_in_copies = [start(y_in.at[y], y_in.at[y], at(y=dy)) for dy in y_parts]
    run(run_s)

    out_total = jnp.zeros((16, PIECE), F32)
    for j in both:
        prod = gc[2 * y + j, own_rows].astype(F32) * fb[j].astype(F32)
        out_total = out_total + dot_t(sel[2 * y + j, 0], prod.astype(BF16))
    y_out[y] = jnp.zeros((16, IMG), F32)
    y_out[y, :, 0:PIECE] = out_total
    y_out_copies = [start(y_out.at[y], y_out.at[y], at(y=dy)) for dy in y_parts]
    for copy in y_in_copies + y_out_copies:
        copy.wait_recv()
    s_send[0] = (y_in[0] + y_in[1]) + (y_in[2] + y_in[3])
    s_send[1] = (y_out[0] + y_out[1]) + (y_out[2] + y_out[3])
    last = start_swap(s_send, s_recv)
    for copy in mh_copies:
        copy.wait_recv()
    fin_mid[...] = jnp.concatenate([mh_all[0, 0:4, 0:HALF], mh_all[1, 0:4, 0:HALF]], axis=1)
    fin_hid[...] = jnp.concatenate([mh_all[0, 16:20, 0:HALF], mh_all[1, 16:20, 0:HALF]], axis=1)
    for j in both:
        finals[j].wait_recv()
        factor = dot(own_col[...], sel[2 * dp + j, 1])
        lo[:, lanes[j]] = (
            tok[:, lanes[j]].astype(F32) + bo_in[j].astype(F32) * factor
        ).astype(BF16)
    last.wait_recv()
    fin_in[...] = s_recv[0, 0:4, 0:PIECE] / in_fast[...].astype(F32)
    fin_out[...] = s_recv[1, 0:4, 0:PIECE]
    drain(sends)


def exchange(*arrays):
    vmem = pl.BlockSpec(memory_space=pltpu.VMEM)
    smem = pl.BlockSpec(memory_space=pltpu.SMEM)
    out_shape = [
        jax.ShapeDtypeStruct((PIECE, 2 * IMG), BF16),
        jax.ShapeDtypeStruct((D_BLK, FFB), BF16),
        jax.ShapeDtypeStruct((D_BLK, FFB), BF16),
        jax.ShapeDtypeStruct((4, PIECE), F32),
        jax.ShapeDtypeStruct((4, PIECE), F32),
        jax.ShapeDtypeStruct((4, FFB), F32),
        jax.ShapeDtypeStruct((4, FFB), F32),
    ]
    scratch = [
        ((N_IMG, D_BLK, IMG), BF16),
        ((N_IMG, D_BLK, IMG), BF16),
        ((N_IMG, D_BLK, IMG), BF16),
        ((N_IMG, D_BLK, IMG), BF16),
        ((FFB, FFB), BF16),
        ((16, FFB), F32),
        ((16, IMG), BF16),
        ((FFB, 16), BF16),
        ((8, 16, IMG), BF16),
        ((D_BLK, 16), BF16),
        ((PIECE, 16), BF16),
        ((N_IMG, 2, 16, IMG), BF16),
        ((16, 128), F32),
        ((4, N_IMG, 8, IMG), F32),
        ((D_BLK, 128), F32),
        ((2, N_IMG, HALF, IMG), F32),
        ((2, N_IMG, HALF, IMG), BF16),
        ((2, N_IMG, HALF, IMG), BF16),
        ((2, N_IMG, HALF, IMG), BF16),
        ((2, N_IMG, HALF, IMG), BF16),
        ((N_IMG, FFB, IMG), BF16),
        ((N_IMG, FFB, IMG), BF16),
        ((2, 2, 2, PAIR, IMG), BF16),
        ((2, 2, 4, PAIR, IMG), BF16),
        ((2, 2, PIECE, IMG), BF16),
        ((2, 2, PAIR, IMG), BF16),
        ((2, PIECE, IMG), BF16),
        ((2, PIECE, IMG), BF16),
        ((2, PIECE, IMG), BF16),
        ((8, 16, IMG), F32),
        ((7, 16, IMG), F32),
        ((4, 16, IMG), F32),
        ((4, 16, IMG), F32),
        ((2, 16, IMG), F32),
        ((2, 16, IMG), F32),
        ((32, IMG), F32),
        ((4, 32, IMG), F32),
    ]
    return pl.pallas_call(
        kernel,
        out_shape=out_shape,
        in_specs=[vmem, vmem, smem] + [vmem] * 6,
        out_specs=[vmem] * 7,
        scratch_shapes=[pltpu.VMEM(s, d) for s, d in scratch]
        + [pltpu.SemaphoreType.DMA((N_SEM,)), pltpu.SemaphoreType.DMA((N_SEM,))],
        compiler_params=pltpu.CompilerParams(
            collective_id=0, has_side_effects=True, vmem_limit_bytes=62 * 1024 * 1024
        ),
        cost_estimate=pl.CostEstimate(
            flops=14_500_000_000, bytes_accessed=12_000_000, transcendentals=1_600_000
        ),
    )(*arrays)


def body(
    tokens, member, up_weight, down_weight, in_fast, hidden_fast, mid_fast, out_fast, cotangent
):
    lo, ug, dg, in_grad, out_grad, mid_grad, hidden_grad = exchange(
        tokens.T, cotangent.T, member, in_fast, out_fast, hidden_fast, mid_fast,
        up_weight, down_weight,
    )
    return (lo.T, ug.astype(F32), dg.astype(F32), in_grad, hidden_grad, mid_grad, out_grad)


def solution(mesh):
    grid = Mesh(mesh.devices.reshape([SIZES[a] for a in AXES]), AXES)
    dp, mp = ("h", "c"), ("y", "x", "l")
    in_specs = (
        P(dp, mp),
        P(dp),
        P(dp, mp),
        P(dp, mp),
        P(None, mp),
        P(None, mp),
        P(None, mp),
        P(None, mp),
        P(dp, mp),
    )
    out_specs = (
        P(dp, mp),
        P(dp, mp),
        P(dp, mp),
        P(None, mp),
        P(None, mp),
        P(None, mp),
        P(None, mp),
    )
    return jax.shard_map(body, mesh=grid, in_specs=in_specs, out_specs=out_specs, check_vma=False)
```

time: 220 us -> 159 us (0.72)
  Pallas kernels: 197 us -> 150 us
  local copies, waits for them, and re-layouts: 13.6 us -> 3.07 us
  other arithmetic: 7.32 us -> 4.48 us
    pallas_call x1, Pallas kernels: 197 us -> 150 us  [exchange(): pl.pallas_call(kernel, out_shape=out_shape, in_specs=[vmem, vmem, smem] +...]
    unnamed x10 -> x17, local copies, waits for them, and re-layouts: 6.5 us -> 3.07 us
    convert_element_type x3 -> x2, other arithmetic: 1.49 us -> 4.48 us  [the longest x1 2.92 us: body(): ug.astype(F32)]
where the time goes in v2:
time: 159 us
  Pallas kernels  150 us (94%)
  other arithmetic  4.48 us (3%)
  local copies, waits for them, and re-layouts  3.07 us (2%)
    pallas_call x1, Pallas kernels, exchange(): pl.pallas_call(kernel, out_shape=out_shape, in_specs=[vmem, vmem, smem] +...  150 us

profile of v2, /device:TPU:16, one launch (start us, length us, event | category | flops | bytes accessed | tf_op | source)
XLA Modules:
  0.0 158.7 jit_solution(11217720351570840773)
XLA Ops:
  0.6 150.5 %shard_map.144 = (bf16[192,512]{1,0:T(8,128)(2,1)}, bf16[1536,384]{1,0:T(8,128)(2,1)}, bf16[1536,384]{1,0:T(8,128)(2,1)}, f32[4,192]{1,0:T(4,128)}, f32[4,192]{1...) custom-call(bf16[192,512]{1,0:T(8,128)(2,1)} %bitcast.4, bf16[192,512]{1,0:T(8,128)(2,1)} %bitcast.5, s32[2]{0:T(128)} %member.1, ...), custom_call_target="tpu_custom_call" | custom-call | flops 14499999744 | bytes 12000000 | tf_op jit(solution)/shard_map/pallas_call | solution.py:656
  151.1 0.0 copy-start
  151.1 2.9 %convert_element_type.6 = f32[1536,384]{1,0:T(8,128)} convert(bf16[1536,384]{1,0:T(8,128)(2,1)} %get-tuple-element.15) | non-fusion elementwise | flops 589824 | bytes 3538944 | tf_op jit(solution)/shard_map/convert_element_type | solution.py:679
  154.1 0.0 copy-done
  154.1 0.0 copy-start.1
  154.1 0.0 copy-start.5
  154.1 0.0 copy-start.3
  154.1 0.0 copy-start.2
  154.1 0.0 copy-start.4
  154.1 1.6 convert_element_type.7
  155.7 0.0 copy-done.1
  155.7 0.7 copy.21
  156.3 0.0 copy-done.5
  156.3 0.6 copy.22
  156.9 0.0 copy-done.3
  156.9 0.6 copy.23
  157.5 0.0 copy-done.2
  157.5 0.6 copy.24
  158.1 0.0 copy-done.4
  158.1 0.6 copy.25
Async XLA Ops:
  151.1 2.9 %copy-start = (bf16[1536,384]{1,0:T(8,128)(2,1)S(1)}, bf16[1536,384]{1,0:T(8,128)(2,1)}, u32[]{:S(2)}) copy-start(bf16[1536,384]{1,0:T(8,128)(2,1)} %get-tuple-element.16) | copy-start | bytes 3538948
  154.1 1.6 %copy-start.1 = (bf16[192,512]{1,0:T(8,128)(2,1)S(1)}, bf16[192,512]{1,0:T(8,128)(2,1)}, u32[]{:S(2)}) copy-start(bf16[192,512]{1,0:T(8,128)(2,1)} %get-tuple-element.14) | copy-start | bytes 589828
  154.1 2.3 %copy-start.5 = (f32[4,192]{1,0:T(4,128)S(1)}, f32[4,192]{1,0:T(4,128)}, u32[]{:S(2)}) copy-start(f32[4,192]{1,0:T(4,128)} %get-tuple-element.31) | copy-start | bytes 9220
  154.1 2.9 %copy-start.3 = (f32[4,384]{1,0:T(4,128)S(1)}, f32[4,384]{1,0:T(4,128)}, u32[]{:S(2)}) copy-start(f32[4,384]{1,0:T(4,128)} %get-tuple-element.32) | copy-start | bytes 18436
  154.1 3.5 %copy-start.2 = (f32[4,384]{1,0:T(4,128)S(1)}, f32[4,384]{1,0:T(4,128)}, u32[]{:S(2)}) copy-start(f32[4,384]{1,0:T(4,128)} %get-tuple-element.33) | copy-start | bytes 18436
  154.1 4.0 %copy-start.4 = (f32[4,192]{1,0:T(4,128)S(1)}, f32[4,192]{1,0:T(4,128)}, u32[]{:S(2)}) copy-start(f32[4,192]{1,0:T(4,128)} %get-tuple-element.34) | copy-start | bytes 9220

commit v3 on v2

--- a/solution.py
+++ b/solution.py
@@ -46,7 +46,7 @@
 def kernel(
     tok, cot, member, in_fast, out_fast, hidden_fast, mid_fast, wu, wd,
     lo, ug, dg, fin_in, fin_out, fin_mid, fin_hid,
-    gx, xn, gc, dc, eye, tab_f, tab_own, hm_col, tabs, tabt, own_col, sel, selm, stats, col,
+    gx, xn, gc, dc, eye, tab_f, tab_own, hm_col, tabs, tabt, own_col, sel, selm, st_own, st_xl, st_y, stats, col,
     pa, p_send, p_recv, h_send, h_recv, hid, upc,
     rf, rv, ruf, ru, rl, fb, bo_in,
     in_acc, in_recv, y_in, y_out, s_send, s_recv, mh_own, mh_all, ss, rs,
@@ -138,7 +138,6 @@
     swap_tab = start_swap(tab_own, tabs.at[own_piece])
     sel_mine = sel.at[pl.ds(2 * dp, 2)]
     sel_copies = [start(sel_mine, sel_mine, dev) for dev in dp_parts]
-    swap_c = [start_swap(cot.at[:, lanes[j]], gc.at[2 * dp + j, own_rows]) for j in (0, 1)]
 
     def image(j, dy):
         return 2 * lax.rem(y + (dy + 4), 4) + j
@@ -159,7 +158,7 @@
 
     both = (0, 1)
 
-    def gather(buf, swaps):
+    def gather(buf, swaps, mate):
         r = [dict(), dict()]
 
         def u_send(j, du, q, step, name):
@@ -170,12 +169,22 @@
             part = chunk(buf, j, du, dv)
             r[j][name] = start(part, part, v_dev(j, step))
 
+        def own_send(j, dv, step, name):
+            piece = chunk(buf, j, 0, dv, l)
+            r[j][name] = start(piece, piece, v_dev(j, step))
+
+        def mate_send(j, dv, name):
+            piece = chunk(buf, j, 0, dv, l)
+            r[j][name] = start(piece, piece, at(l=1))
+
         for j in both:
             swaps[j].wait_recv()
-            piece = chunk(buf, j, 0, 0, l)
-            r[j]["l"] = start(piece, piece, at(l=1))
+            mate_send(j, 0, "l")
             u_send(j, 0, l, 1, "-own")
             u_send(j, 0, l, -1, "+own")
+            if mate:
+                own_send(j, 0, 1, "v-0")
+                own_send(j, 0, -1, "v+0")
         yield
         for j in both:
             r[j]["l"].wait_recv()
@@ -185,8 +194,15 @@
             r[j]["-own"].wait_recv()
             u_send(j, -1, l, 1, "fwd-")
         for j in both:
-            v_send(j, 0, 0, 1, "v-0")
-            v_send(j, 0, 0, -1, "v+0")
+            if mate:
+                r[j]["v-0"].wait_recv()
+                own_send(j, -1, 1, "w-0")
+                mate_send(j, -1, "m-0")
+                r[j]["v+0"].wait_recv()
+                mate_send(j, 1, "m+0")
+            else:
+                v_send(j, 0, 0, 1, "v-0")
+                v_send(j, 0, 0, -1, "v+0")
         yield
         for j in both:
             r[j]["+own"].wait_recv()
@@ -203,28 +219,40 @@
             r[j]["fwd+"].wait_recv()
             v_send(j, 2, 0, 1, "v-2")
             v_send(j, 2, 0, -1, "v+2")
-        yield
-        for j in both:
-            r[j]["v-0"].wait_recv()
-            v_send(j, 0, -1, 1, "w-0")
+        for j in both:
+            if mate:
+                r[j]["w-0"].wait_recv()
+                mate_send(j, 2, "m2")
+        yield
+        for j in both:
+            if not mate:
+                r[j]["v-0"].wait_recv()
+                v_send(j, 0, -1, 1, "w-0")
             r[j]["v+1"].wait_recv()
             v_send(j, 1, 1, -1, "w+1")
-        yield
-        for j in both:
             r[j]["v-m"].wait_recv()
             v_send(j, -1, -1, 1, "w-m")
+        yield
+        for j in both:
             r[j]["v+2"].wait_recv()
             v_send(j, 2, 1, -1, "w+2")
-        yield
-        for name in ("v+0", "v+m", "v-1", "v-2"):
+        for j in both:
+            if mate:
+                r[j]["m-0"].wait_recv()
+                r[j]["m+0"].wait_recv()
+            else:
+                r[j]["v+0"].wait_recv()
+        last_own = "m2" if mate else "w-0"
+        r[1][last_own].wait_recv()
+        yield
+        for name in ("v+m", "v-1", "v-2"):
             for j in both:
                 r[j][name].wait_recv()
-        r[1]["w-0"].wait_recv()
-        yield
-        for name in ("w-0", "w+1", "w-m", "w+2"):
+        r[0][last_own].wait_recv()
+        yield
+        for name in ("w+1", "w-m", "w+2"):
             for j in both:
-                if (j, name) != (1, "w-0"):
-                    r[j][name].wait_recv()
+                r[j][name].wait_recv()
         yield
 
     def run(gen, steps=1000):
@@ -237,27 +265,64 @@
     third = [image(1, -1), image(1, 1), image(0, 2), image(1, 2)]
     order = first + second + third
 
-    run_x = gather(gx, swap_x)
-    run_c = gather(gc, swap_c)
+    run_x = gather(gx, swap_x, True)
+
+    stat_row = lax.broadcasted_iota(jnp.int32, (8, IMG), 0)
+
+    def two_rows(first_row, second_row):
+        return jnp.where(stat_row == 0, first_row, jnp.where(stat_row == 1, second_row, 0.0))
+
+    def combine(parts, count):
+        mean = sum(p[0:1] for p in parts) * (1.0 / len(parts))
+        dev2 = sum(p[1:2] for p in parts)
+        for p in parts:
+            gap = p[0:1] - mean
+            dev2 = dev2 + count * (gap * gap)
+        return mean, dev2
+
+    for j in both:
+        values = tok[:, lanes[j]].astype(F32)
+        mean = jnp.sum(values, axis=0, keepdims=True) * (1.0 / PIECE)
+        gap = values - mean
+        st_own[j] = two_rows(mean, jnp.sum(gap * gap, axis=0, keepdims=True))
+    st_copies = [
+        start(st_own, st_xl.at[i], at(x=dx, l=dl)) for i, (dx, dl) in enumerate(xl_parts)
+    ]
     run(run_x, 1)
 
     swap_tab.wait_recv()
     tab_copies = [
         start(tabs.at[own_piece], tabs.at[own_piece], at(x=dx, l=dl)) for dx, dl in xl_parts
     ]
+    for copy in st_copies:
+        copy.wait_recv()
+    for j in both:
+        st_y[y, j] = two_rows(
+            *combine([st_own[j]] + [st_xl[i, j] for i in range(7)], float(PIECE))
+        )
+    st_copies = [start(st_y.at[y], st_y.at[y], at(y=dy)) for dy in y_parts]
     run(run_x, 1)
+    swap_c = [start_swap(cot.at[:, lanes[j]], gc.at[2 * dp + j, own_rows]) for j in (0, 1)]
+    run_c = gather(gc, swap_c, False)
     ident = lax.broadcasted_iota(jnp.int32, (FFB, FFB), 0) == lax.broadcasted_iota(
         jnp.int32, (FFB, FFB), 1
     )
     eye[...] = jnp.where(ident, 1.0, 0.0).astype(BF16)
     run(run_x, 1)
+    for copy in st_copies:
+        copy.wait_recv()
+    for j in both:
+        mean, dev2 = combine([st_y[k, j] for k in range(4)], float(D_BLK))
+        stats[2 * dp + j] = two_rows(mean, lax.rsqrt(dev2 / (4 * D_BLK) + 1e-06))
+    stat_mine = stats.at[pl.ds(2 * dp, 2)]
+    stat_copies = [start(stat_mine, stat_mine, dev) for dev in dp_parts]
     own_col[...] = dot_t(eye[:PIECE, :IMG], tab_own[...]).astype(BF16)
     tab_f[0:4, :] = hidden_fast[...].astype(F32)
     tab_f[8:12, :] = mid_fast[...].astype(F32)
     hm_col[...] = dot_t(eye[...], tab_f[...].astype(BF16)).astype(BF16)
     col[...] = jnp.zeros((D_BLK, 128), F32)
     run(run_x, 1)
-    for copy in sel_copies:
+    for copy in sel_copies + stat_copies:
         copy.wait_recv()
     for copy in tab_copies:
         copy.wait_recv()
@@ -269,40 +334,9 @@
         picks = jnp.where(lane == img, sel[img, 0][:, 0:128].astype(F32), picks)
     selm[...] = picks
 
-    stat_copies = {}
-    stat_row = lax.broadcasted_iota(jnp.int32, (8, IMG), 0)
-
-    def image_stats(n):
-        img = order[n]
-
-        def total(p, acc):
-            rows = pl.ds(pl.multiple_of(p * PIECE, PIECE), PIECE)
-            v = gx[img, rows].astype(F32).reshape(PIECE // 8, 8, IMG)
-            return acc + jnp.sum(v, axis=0)
-
-        def spread(p, acc):
-            rows = pl.ds(pl.multiple_of(p * PIECE, PIECE), PIECE)
-            v = (gx[img, rows].astype(F32) - mean).reshape(PIECE // 8, 8, IMG)
-            return acc + jnp.sum(v * v, axis=0)
-
-        zero = jnp.zeros((8, IMG), F32)
-        mean = jnp.sum(lax.fori_loop(0, 8, total, zero), axis=0, keepdims=True) / D_BLK
-        dev2 = jnp.sum(lax.fori_loop(0, 8, spread, zero), axis=0, keepdims=True)
-        stats[dp, img] = jnp.where(stat_row == 0, mean, jnp.where(stat_row == 1, dev2, 0.0))
-        part = stats.at[dp, img]
-        stat_copies[n] = [start(part, part, dev) for dev in dp_parts]
-
     def normalise(n):
         img = order[n]
-        for copy in stat_copies[n]:
-            copy.wait_recv()
-        parts = [stats[k, img] for k in range(4)]
-        mean = (parts[0][0:1] + parts[1][0:1] + parts[2][0:1] + parts[3][0:1]) * 0.25
-        dev2 = parts[0][1:2] + parts[1][1:2] + parts[2][1:2] + parts[3][1:2]
-        for k in range(4):
-            gap = parts[k][0:1] - mean
-            dev2 = dev2 + D_BLK * (gap * gap)
-        rstd = lax.rsqrt(dev2 / (4 * D_BLK) + 1e-06)
+        mean, rstd = stats[img, 0:1], stats[img, 1:2]
         factor = dot(tabt[...], sel[img, 0])
         xn[img] = ((gx[img].astype(F32) - mean) * rstd * factor).astype(BF16)
 
@@ -355,45 +389,55 @@
         normalise(n)
         partial_product(0, wu, xn, n)
 
-    run(run_x, 2)
-    image_stats(0)
+    def backward(n):
+        img = order[n]
+        factor = dot(tabt[...], sel[img, 1])
+        dc[img] = (gc[img].astype(F32) * factor).astype(BF16)
+        partial_product(1, wd, dc, n)
+
+    def each(step, *numbers):
+        for n in numbers:
+            step(n)
+
+    forward(0)
+    run(run_x, 1)
+    to_far(0, 0)
+    run(run_x, 1)
+    forward(1)
     run(run_c, 1)
+    to_far(0, 1)
     run(run_x, 1)
-    for n in (1, 2, 3):
-        image_stats(n)
-    forward(0)
-    run(run_c, 1)
-    forward(1)
-    to_far(0, 0)
+    forward(2)
+    forward(3)
+    to_far(0, 2)
+    to_far(0, 3)
     run(run_x, 1)
     x_sends = list(sends)
     sends.clear()
-    for n in (4, 5, 6, 7):
-        image_stats(n)
-    forward(2)
-    to_far(0, 1)
-    forward(3)
-    to_far(0, 2)
     run(run_c, 1)
-    finish_hidden(0)
-    for n in (4, 5, 6, 7):
-        forward(n)
-        to_far(0, n - 1)
-        finish_hidden(n - 3)
+    forward(4)
+    forward(5)
+    to_far(0, 4)
+    forward(6)
+    to_far(0, 5)
+    forward(7)
+    to_far(0, 6)
+    to_far(0, 7)
     run(run_c, 1)
-    to_far(0, 7)
+    each(finish_hidden, 0, 1, 2, 3)
+    run(run_c, 1)
+    drain(x_sends)
+    each(branch_part, 0, 1, 2, 3)
+    finish_hidden(4)
+    run(run_c, 1)
     finish_hidden(5)
-    drain(x_sends)
+    branch_part(4)
+    finish_hidden(6)
+    branch_part(5)
     run(run_c, 1)
-    for n in (0, 1, 2):
-        branch_part(n)
-    finish_hidden(6)
-    for n in (3, 4, 5):
-        branch_part(n)
     finish_hidden(7)
-    run(run_c, 1)
-    for n in (6, 7):
-        branch_part(n)
+    branch_part(6)
+    branch_part(7)
 
     up, down = (0, -1), (1, 2)
     slot = {0: 0, -1: 1, 1: 2, 2: 3}
@@ -476,12 +520,6 @@
 
     run_s = scatter()
     run(run_s, 1)
-
-    def backward(n):
-        img = order[n]
-        factor = dot(tabt[...], sel[img, 1])
-        dc[img] = (gc[img].astype(F32) * factor).astype(BF16)
-        partial_product(1, wd, dc, n)
 
     mh_own[...] = jnp.zeros((32, IMG), F32)
 
@@ -518,41 +556,37 @@
         ug[rows, :] = acc.astype(BF16)
 
     backward(0)
+    backward(1)
+    to_far(1, 0)
     run(run_c, 1)
-    to_far(1, 0)
-    for n in (1, 2, 3):
-        backward(n)
-        if n > 1:
-            to_far(1, n - 1)
+    backward(2)
+    to_far(1, 1)
+    backward(3)
+    to_far(1, 2)
     run(run_c, 1)
-    to_far(1, 3)
     for n in (4, 5, 6, 7):
         backward(n)
-        if n > 4:
-            to_far(1, n - 1)
-        finish_cot(n - 4)
+        to_far(1, n - 1)
     to_far(1, 7)
     run(run_s, 1)
+    each(finish_cot, 0, 1)
+    run(run_s, 1)
+    each(finish_cot, 2, 3)
     down_rows(0)
     finish_cot(4)
+    down_rows(1)
     run(run_s, 1)
-    down_rows(1)
-    finish_cot(5)
-    down_rows(2)
-    finish_cot(6)
-    down_rows(3)
-    finish_cot(7)
+    each(finish_cot, 5, 6, 7)
     mh_all[dp] = mh_own[...]
     mh_copies = [start(mh_own, mh_all.at[dp], dev) for dev in dp_parts]
+    down_rows(2)
+    run(run_s, 1)
+    down_rows(3)
     for n in range(8):
         upc_copies[n].wait_recv()
     up_rows(0)
     run(run_s, 1)
-    up_rows(1)
-    up_rows(2)
-    run(run_s, 1)
-    up_rows(3)
-    run(run_s, 1)
+    each(up_rows, 1, 2, 3)
 
     in_acc[...] = jnp.zeros((8, 16, IMG), F32)
     for p in range(8):
@@ -602,6 +636,31 @@
     drain(sends)
 
 
+def widen(ug, dg, lo, *small):
+    def copy(*refs):
+        n = len(refs) // 2
+        for src, dst in zip(refs[:n], refs[n:]):
+            dst[...] = src[...].astype(dst.dtype)
+
+    def spec(a, split):
+        if split:
+            return pl.BlockSpec((a.shape[0] // 4, a.shape[1]), lambda i: (i, 0))
+        return pl.BlockSpec(a.shape, lambda i: (0, 0))
+
+    arrays = (ug, dg, lo) + small
+    specs = [spec(a, n < 2) for n, a in enumerate(arrays)]
+    return pl.pallas_call(
+        copy,
+        grid=(4,),
+        in_specs=specs,
+        out_specs=specs,
+        out_shape=[
+            jax.ShapeDtypeStruct(a.shape, F32 if n < 2 else a.dtype)
+            for n, a in enumerate(arrays)
+        ],
+    )(*arrays)
+
+
 def exchange(*arrays):
     vmem = pl.BlockSpec(memory_space=pltpu.VMEM)
     smem = pl.BlockSpec(memory_space=pltpu.SMEM)
@@ -628,7 +687,10 @@
         ((PIECE, 16), BF16),
         ((N_IMG, 2, 16, IMG), BF16),
         ((16, 128), F32),
-        ((4, N_IMG, 8, IMG), F32),
+        ((2, 8, IMG), F32),
+        ((7, 2, 8, IMG), F32),
+        ((4, 2, 8, IMG), F32),
+        ((N_IMG, 8, IMG), F32),
         ((D_BLK, 128), F32),
         ((2, N_IMG, HALF, IMG), F32),
         ((2, N_IMG, HALF, IMG), BF16),
@@ -676,7 +738,10 @@
         tokens.T, cotangent.T, member, in_fast, out_fast, hidden_fast, mid_fast,
         up_weight, down_weight,
     )
-    return (lo.T, ug.astype(F32), dg.astype(F32), in_grad, hidden_grad, mid_grad, out_grad)
+    ug, dg, lo, in_grad, out_grad, mid_grad, hidden_grad = widen(
+        ug, dg, lo, in_grad, out_grad, mid_grad, hidden_grad
+    )
+    return (lo.T, ug, dg, in_grad, hidden_grad, mid_grad, out_grad)
 
 
 def solution(mesh):

time: 159 us -> 152 us (0.956)
  other arithmetic: 4.48 us -> 0 us
  local copies, waits for them, and re-layouts: 3.07 us -> 0 us
    pallas_call x1, Pallas kernels: 150 us -> 145 us  [exchange(): pl.pallas_call(kernel, out_shape=out_shape, in_specs=[vmem, vmem, smem] +...]
    convert_element_type x2 -> x0, other arithmetic: 4.48 us -> none  [the longest x1 2.92 us: body(): ug.astype(F32)]
    pallas_call x0 -> x1, Pallas kernels: none -> 4.46 us  [widen(): pl.pallas_call(copy, grid=(4,), in_specs=specs, out_specs=specs, out_shap...]
    unnamed x17 -> x0, local copies, waits for them, and re-layouts: 3.07 us -> none
where the time goes in v3:
time: 152 us; the launch traced here: 150 us
  Pallas kernels  150 us (99%)
    pallas_call x1, Pallas kernels, exchange(): pl.pallas_call(kernel, out_shape=out_shape, in_specs=[vmem, vmem, smem] +...  145 us
    pallas_call x1, Pallas kernels, widen(): pl.pallas_call(copy, grid=(4,), in_specs=specs, out_specs=specs, out_shap...  4.46 us

profile of v3, /device:TPU:16, one launch (start us, length us, event | category | flops | bytes accessed | tf_op | source)
XLA Modules:
  0.0 150.4 jit_solution(5968130758696396328)
XLA Ops:
  0.6 145.2 %shard_map.144 = (bf16[192,512]{1,0:T(8,128)(2,1)}, bf16[1536,384]{1,0:T(8,128)(2,1)}, bf16[1536,384]{1,0:T(8,128)(2,1)}, f32[4,192]{1,0:T(4,128)}, f32[4,192]{1...) custom-call(bf16[192,512]{1,0:T(8,128)(2,1)} %bitcast.3, bf16[192,512]{1,0:T(8,128)(2,1)} %bitcast.4, s32[2]{0:T(128)} %member.1, ...), custom_call_target="tpu_custom_call" | custom-call | flops 14499999744 | bytes 12000000 | tf_op jit(solution)/shard_map/pallas_call | solution.py:718
  145.9 4.5 %shard_map.145 = (f32[1536,384]{1,0:T(8,128)}, f32[1536,384]{1,0:T(8,128)}, bf16[192,512]{1,0:T(8,128)(2,1)}, f32[4,192]{1,0:T(4,128)}, f32[4,192]{1,0:T(4,128)}, /*index=5*/f32[4,384]{1,0:T(4,128)}, f32[4,384]{1,0:T(4,128)}) custom-call(bf16[1536,384]{1,0:T(8,128)(2,1)} %get-tuple-element.21.refs_0_, bf16[1536,384]{1,0:T(8,128)(2,1)} %get-tuple-element.22.refs_1_, ...), custom_call_target="tpu_custom_call" | custom-call | tf_op jit(solution)/shard_map/pallas_call | solution.py:652

commit v4 on v3

--- a/solution.py
+++ b/solution.py
@@ -586,7 +586,9 @@
         upc_copies[n].wait_recv()
     up_rows(0)
     run(run_s, 1)
-    each(up_rows, 1, 2, 3)
+    up_rows(1)
+    run(run_s, 1)
+    each(up_rows, 2, 3)
 
     in_acc[...] = jnp.zeros((8, 16, IMG), F32)
     for p in range(8):
@@ -598,7 +600,6 @@
     for i, (dx, dl) in enumerate(xl_parts):
         p_to = 2 * lax.rem(x + dx, 4) + lax.rem(l + dl, 2)
         in_copies.append(start(in_acc.at[p_to], in_recv.at[i], at(x=dx, l=dl)))
-    run(run_s, 1)
     for copy in in_copies:
         copy.wait_recv()
     total_in = in_acc[own_piece]

time: 152 us -> 150 us (0.987); the launches traced: 150 us -> 150 us
  no operation moved by 1% of the time
where the time goes in v4:
time: 150 us
  Pallas kernels  149 us (99%)
    pallas_call x1, Pallas kernels, exchange(): pl.pallas_call(kernel, out_shape=out_shape, in_specs=[vmem, vmem, smem] +...  145 us
    pallas_call x1, Pallas kernels, widen(): pl.pallas_call(copy, grid=(4,), in_specs=specs, out_specs=specs, out_shap...  4.46 us

profile of v4, /device:TPU:16, one launch (start us, length us, event | category | flops | bytes accessed | tf_op | source)
XLA Modules:
  0.0 150.1 jit_solution(13069819063993350735)
XLA Ops:
  0.6 145.0 %shard_map.144 = (bf16[192,512]{1,0:T(8,128)(2,1)}, bf16[1536,384]{1,0:T(8,128)(2,1)}, bf16[1536,384]{1,0:T(8,128)(2,1)}, f32[4,192]{1,0:T(4,128)}, f32[4,192]{1...) custom-call(bf16[192,512]{1,0:T(8,128)(2,1)} %bitcast.3, bf16[192,512]{1,0:T(8,128)(2,1)} %bitcast.4, s32[2]{0:T(128)} %member.1, ...), custom_call_target="tpu_custom_call" | custom-call | flops 14499999744 | bytes 12000000 | tf_op jit(solution)/shard_map/pallas_call | solution.py:719
  145.6 4.5 %shard_map.145 = (f32[1536,384]{1,0:T(8,128)}, f32[1536,384]{1,0:T(8,128)}, bf16[192,512]{1,0:T(8,128)(2,1)}, f32[4,192]{1,0:T(4,128)}, f32[4,192]{1,0:T(4,128)}, /*index=5*/f32[4,384]{1,0:T(4,128)}, f32[4,384]{1,0:T(4,128)}) custom-call(bf16[1536,384]{1,0:T(8,128)(2,1)} %get-tuple-element.21.refs_0_, bf16[1536,384]{1,0:T(8,128)(2,1)} %get-tuple-element.22.refs_1_, ...), custom_call_target="tpu_custom_call" | custom-call | tf_op jit(solution)/shard_map/pallas_call | solution.py:653

commit v5 on v4

--- a/solution.py
+++ b/solution.py
@@ -645,14 +645,14 @@
 
     def spec(a, split):
         if split:
-            return pl.BlockSpec((a.shape[0] // 4, a.shape[1]), lambda i: (i, 0))
+            return pl.BlockSpec((a.shape[0] // 2, a.shape[1]), lambda i: (i, 0))
         return pl.BlockSpec(a.shape, lambda i: (0, 0))
 
     arrays = (ug, dg, lo) + small
-    specs = [spec(a, n < 2) for n, a in enumerate(arrays)]
+    specs = [spec(a, n < 3) for n, a in enumerate(arrays)]
     return pl.pallas_call(
         copy,
-        grid=(4,),
+        grid=(2,),
         in_specs=specs,
         out_specs=specs,
         out_shape=[

time: 150 us -> 150 us (level)
  no operation moved by 1% of the time
where the time goes in v5:
time: 150 us
  Pallas kernels  149 us (99%)
    pallas_call x1, Pallas kernels, exchange(): pl.pallas_call(kernel, out_shape=out_shape, in_specs=[vmem, vmem, smem] +...  145 us
    pallas_call x1, Pallas kernels, widen(): pl.pallas_call(copy, grid=(2,), in_specs=specs, out_specs=specs, out_shap...  3.8 us

profile of v5, /device:TPU:16, one launch (start us, length us, event | category | flops | bytes accessed | tf_op | source)
XLA Modules:
  0.0 149.6 jit_solution(14414710707471588336)
XLA Ops:
  0.6 145.0 %shard_map.144 = (bf16[192,512]{1,0:T(8,128)(2,1)}, bf16[1536,384]{1,0:T(8,128)(2,1)}, bf16[1536,384]{1,0:T(8,128)(2,1)}, f32[4,192]{1,0:T(4,128)}, f32[4,192]{1...) custom-call(bf16[192,512]{1,0:T(8,128)(2,1)} %bitcast.3, bf16[192,512]{1,0:T(8,128)(2,1)} %bitcast.4, s32[2]{0:T(128)} %member.1, ...), custom_call_target="tpu_custom_call" | custom-call | flops 14499999744 | bytes 12000000 | tf_op jit(solution)/shard_map/pallas_call | solution.py:719
  145.6 3.8 %shard_map.145 = (f32[1536,384]{1,0:T(8,128)}, f32[1536,384]{1,0:T(8,128)}, bf16[192,512]{1,0:T(8,128)(2,1)}, f32[4,192]{1,0:T(4,128)}, f32[4,192]{1,0:T(4,128)}, /*index=5*/f32[4,384]{1,0:T(4,128)}, f32[4,384]{1,0:T(4,128)}) custom-call(bf16[1536,384]{1,0:T(8,128)(2,1)} %get-tuple-element.21.refs_0_, bf16[1536,384]{1,0:T(8,128)(2,1)} %get-tuple-element.22.refs_1_, ...), custom_call_target="tpu_custom_call" | custom-call | tf_op jit(solution)/shard_map/pallas_call | solution.py:653
